TPU v7x, 32 devices: a whole 2x2x4 slice. The times are simulated.
32 devices in a mesh: row: 8 (over z, y), col: 4 (over x, core).
Axes of the slice: x: 2, y: 2, z: 4, core: 2. Of those that a mesh axis runs over, the one named last changes fastest.
Arguments:
- panel: float32 [8, 8, 256, 256], P(None, 'row', None, 'col'), may hold values from -0.1875 to 0.1875
- slab: bfloat16 [8, 8, 256, 4, 4, 256], P(None, 'row', None, None, 'col'), may hold values from -6 to 6
- cotangent: bfloat16 [8, 8, 256, 4, 4, 256], P(None, 'row', None, None, 'col'), may hold values from -0.0625 to 0.0625
- inverse: float32 [256, 256], replicated, may hold values from -2 to 8, as said below
Outputs:
- updated: bfloat16 [8, 8, 256, 4, 4, 256], P(None, 'row', None, None, 'col')
- grad_panel: float32 [8, 8, 256, 256], P(None, 'row', None, 'col')
- grad_inverse: float32 [256, 256], P(None, 'col')
Inputs may be any that keep to these rules, and one draw needn't show every extreme that they name: `inverse`: lower triangular; diagonal entries between 4 and 8.
All inputs are finite; a program needn't handle non-finite values.
Results may differ from a plain program's by a relative error of at most 0.015.
Values may be sent and summed in bfloat16 or wider, within the bound.
No kernel may reach another device: no remote copies, remote signals or barrier semaphores. Data moves between devices by JAX's collectives and lax.ppermute only.
A program may use at most 128 MiB of HBM per device.

v0:
```python
import functools

import jax
import jax.numpy as jnp
from jax import lax
from jax.experimental import pallas as pl
from jax.experimental.pallas import tpu as pltpu
from jax.sharding import PartitionSpec as P

BOTH = ("row", "col")
F32 = jnp.float32
BF16 = jnp.bfloat16
LANES = 128
VMEM = pl.BlockSpec(memory_space=pltpu.VMEM)
SMEM = pl.BlockSpec(memory_space=pltpu.SMEM)
STREAMED = 58
ANY = pl.BlockSpec(memory_space=pl.ANY)


def bits_of(count):
    return [1 << b for b in reversed(range(count.bit_length() - 1))]


def reversed_bits(value, count):
    width = count.bit_length() - 1
    place = 0
    for b in range(width):
        place = place + (((value >> b) & 1) << (width - 1 - b))
    return place


def dot(a, b, dims, precision=None):
    return lax.dot_general(a, b, (dims, ((), ())), precision=precision, preferred_element_type=F32)


def whole(shape):
    return pl.BlockSpec(shape, lambda *_: (0,) * len(shape))


def params(mib=24):
    return pltpu.CompilerParams(vmem_limit_bytes=mib * 2**20)


def cost(flops, nbytes):
    return pl.CostEstimate(flops=flops, bytes_accessed=nbytes, transcendentals=0)


def unmix_kernel(slabs, tile, inv_ref, x_ref, o_ref, m_ref, wide_ref, ins, outs, in_sems, out_sems):
    step, steps = pl.program_id(0), ins.shape[0]
    size = ins.shape[1]

    def copy_in(t):
        at = pl.multiple_of(t * size, size)
        return pltpu.make_async_copy(x_ref.at[pl.ds(at, size)], ins.at[t], in_sems.at[t])

    def copy_out(t):
        at = pl.multiple_of(t * tile, tile)
        return pltpu.make_async_copy(outs.at[t], o_ref.at[pl.ds(at, tile)], out_sems.at[t])

    @pl.when(step == 0)
    def _():
        for t in range(steps):
            copy_in(t).start()
        mat = dot(inv_ref[...], inv_ref[...], ((0,), (0,)), lax.Precision.HIGHEST)
        high = mat.astype(BF16)
        m_ref[0] = high
        m_ref[1] = (mat - high.astype(F32)).astype(BF16)

    copy_in(step).wait()
    halves = tile // LANES
    wide_ref[...] = ins[step].astype(F32)
    for s in range(slabs):
        for h in range(halves):
            part = wide_ref[pl.ds(h * slabs + s, tile, stride=halves * slabs), :]
            outs[step, :, s * tile + h * LANES : s * tile + (h + 1) * LANES] = part.astype(BF16)
    copy_out(step).start()

    @pl.when(step == steps - 1)
    def _():
        for t in range(steps):
            copy_out(t).wait()


def q_kernel(n_row, n_col, groups, place_ref, *refs):
    parts, (m_ref, g_ref, q_ref, e_ref, pt_ref, ins, sems) = refs[:n_col], refs[n_col:]
    tiles, strip, tile = parts[0].shape
    s = pl.program_id(0)
    row, col = place_ref[0], place_ref[1]
    group, rho = row // n_col, (row % n_col) ^ (n_col // 2)

    def copy_in(at):
        columns = pl.ds(pl.multiple_of(at * tile, tile), tile)
        return pltpu.make_async_copy(g_ref.at[:, columns], ins.at[at], sems.at[at])

    @pl.when(s == 0)
    def _():
        for at in range(ins.shape[0]):
            copy_in(at).start()
        for q in range(n_col):
            at = pl.multiple_of((col ^ q) * strip, strip)
            for t in range(tiles):
                pt_ref[pl.ds(at, strip), t * tile : (t + 1) * tile] = parts[q][t]

    copy_in(s).wait()
    q_ref[s] = dot(pt_ref[...], ins[s], ((1,), (0,))).astype(BF16)

    @pl.when(s == pl.num_programs(0) - 1)
    def _():
        for at in range(q_ref.shape[0]):
            q_val = q_ref[at]
            e_val = -(dot(m_ref[0], q_val, ((1,), (0,))) + dot(m_ref[1], q_val, ((1,), (0,))))
            e_val = e_val.astype(BF16)
            slot, other = at // groups, group ^ (at % groups)
            for r in range(n_col):
                place = reversed_bits(rho ^ r, n_col) * groups + other
                e_ref[place, slot] = e_val[r * strip : (r + 1) * strip]


def w_kernel(n_row, n_col, groups, place_ref, *refs):
    tops, (m_ref, inv_ref, q_ref, w_ref, gi_ref, top_all) = refs[:2], refs[2:]
    slots, strip, tile = tops[0].shape[1:]
    half = tops[0].shape[0]
    slabs = slots * groups
    row, col = place_ref[0], place_ref[1]
    group, rho = row // n_col, (row % n_col) ^ (n_col // 2)
    for p in range(n_row):
        at = pl.multiple_of((rho ^ (p % n_col)) * strip, strip)
        place = reversed_bits(p % n_col, n_col) * groups + p // n_col
        for slot in range(slots):
            s = slot * groups + (group ^ (p // n_col))
            top_all[s, pl.ds(at, strip), :] = tops[place // half][place % half, slot]
    z = jnp.zeros((tile, tile), F32)
    for s in range(slabs):
        top = top_all[s]
        w = dot(m_ref[0], top, ((1,), (0,))) + dot(m_ref[1], top, ((1,), (0,)))
        w_ref[:, s * tile : (s + 1) * tile] = w.astype(BF16)
        z = z + dot(top, q_ref[s], ((1,), (1,)))
    z = z + z.T
    gi = -dot(z, inv_ref[...], ((1,), (1,)), lax.Precision.HIGHEST)
    for r in range(n_col):
        gi_ref[col ^ r] = gi[r * strip : (r + 1) * strip].astype(BF16)


def h_kernel(n_col, place_ref, w_ref, g_ref, h_ref):
    strip = h_ref.shape[2]
    t = pl.program_id(0)
    col = place_ref[1]
    h = -dot(w_ref[...], g_ref[...], ((1,), (1,)))
    for r in range(n_col):
        h_ref[reversed_bits(col ^ r, n_col), t] = h[r * strip : (r + 1) * strip].astype(BF16)


def update_kernel(slabs, tile, pt_ref, w_ref, x_ref, *refs):
    o_ref, wide_ref = refs[-2:]
    halves = tile // LANES
    product = dot(pt_ref[...], w_ref[...], ((0,), (0,)))
    for s in range(slabs):
        for h in range(halves):
            part = product[:, s * tile + h * LANES : s * tile + (h + 1) * LANES]
            wide_ref[pl.ds(h * slabs + s, tile, stride=halves * slabs), :] = part
    o_ref[...] = (x_ref[...].astype(F32) - wide_ref[...]).astype(BF16)


def mixed_rows(x):
    tiles, _, tile, slabs, _, _ = x.shape
    x = x.reshape(tiles, tile, slabs, tile // LANES, LANES).transpose(0, 1, 3, 2, 4)
    return x.reshape(-1, LANES)


def per_device(panel, slab, cotangent, inverse):
    tiles, _, tile, strip = panel.shape
    slabs = slab.shape[3]
    n_row = lax.axis_size("row")
    n_col = lax.axis_size("col")
    groups = n_row // n_col
    slots = slabs // groups
    width = slabs * tile
    rows = tiles * tile
    mixed = tile * width // LANES
    place = jnp.stack([lax.axis_index("row"), lax.axis_index("col")]).astype(jnp.int32)

    def permute_row(value, bit):
        return lax.ppermute(value, "row", [(i, i ^ bit) for i in range(n_row)])

    def permute_col(value, bit):
        return lax.ppermute(value, "col", [(i, i ^ bit) for i in range(n_col)])

    far = n_col // 2

    def transpose(value, across, back=False):
        pairs = []
        for m in range(groups):
            for a in range(n_col):
                for b in range(n_col):
                    here = (m * n_col + a) * n_col + b
                    there = ((m ^ across) * n_col + (b ^ far)) * n_col + a
                    pairs.append((there, here) if back else (here, there))
        return lax.ppermute(value, BOTH, pairs)

    own = panel.reshape(tiles, tile, strip).transpose(0, 2, 1).astype(BF16)
    high, *lower = bits_of(n_col)
    parts = {0: own, high: permute_col(own, high)}
    tops = [transpose(own[:slots], m) for m in range(groups)]
    cot, mat = pl.pallas_call(
        functools.partial(unmix_kernel, slabs, tile),
        grid=(tiles,),
        in_specs=[whole((tile, tile)), ANY],
        out_specs=[ANY, whole((2, tile, tile))],
        out_shape=[
            jax.ShapeDtypeStruct((rows, width), BF16),
            jax.ShapeDtypeStruct((2, tile, tile), BF16),
        ],
        scratch_shapes=[
            pltpu.VMEM((mixed, LANES), F32),
            pltpu.VMEM((tiles, mixed, LANES), BF16),
            pltpu.VMEM((tiles, tile, width), BF16),
            pltpu.SemaphoreType.DMA((tiles,)),
            pltpu.SemaphoreType.DMA((tiles,)),
        ],
        compiler_params=params(STREAMED),
        cost_estimate=cost(0, 4 * rows * width),
    )(inverse, mixed_rows(cotangent))

    tops, own, mat = lax.optimization_barrier((tops, own, mat))

    top = jnp.stack(tops)
    for bit in bits_of(n_col)[:-1]:
        top = jnp.concatenate([top, permute_row(top, bit)], 0)
    if lower:
        parts[1] = permute_col(own, 1)
    top, parts = lax.optimization_barrier((top, parts))

    for bit in lower:
        for q in range(0, n_col, 2 * bit):
            if q | bit not in parts:
                parts[q | bit] = permute_col(parts[q], bit)
    tops = [top, permute_row(top, 1)]

    q_sum, e_part, panel_all = pl.pallas_call(
        functools.partial(q_kernel, n_row, n_col, groups),
        grid=(slabs,),
        in_specs=[SMEM]
        + [whole((tiles, strip, tile))] * n_col
        + [whole((2, tile, tile)), ANY],
        out_specs=[
            whole((slabs, tile, tile)),
            whole((n_row, slots, strip, tile)),
            whole((tile, rows)),
        ],
        out_shape=[
            jax.ShapeDtypeStruct((slabs, tile, tile), BF16),
            jax.ShapeDtypeStruct((n_row, slots, strip, tile), BF16),
            jax.ShapeDtypeStruct((tile, rows), BF16),
        ],
        scratch_shapes=[
            pltpu.VMEM((slabs, rows, tile), BF16),
            pltpu.SemaphoreType.DMA((slabs,)),
        ],
        compiler_params=params(STREAMED - 10),
        cost_estimate=cost(2 * rows * width * tile, 2 * rows * (width + tile)),
    )(place, *[parts[q] for q in range(n_col)], mat, cot)

    w, gi = pl.pallas_call(
        functools.partial(w_kernel, n_row, n_col, groups),
        in_specs=[SMEM] + [VMEM] * 5,
        out_specs=[VMEM, VMEM],
        out_shape=[
            jax.ShapeDtypeStruct((tile, width), BF16),
            jax.ShapeDtypeStruct((n_col, strip, tile), BF16),
        ],
        scratch_shapes=[pltpu.VMEM((slabs, tile, tile), BF16)],
        compiler_params=params(),
        cost_estimate=cost(tile, tile),
    )(place, *tops, mat, inverse, q_sum)

    def h_part(first, count):
        return pl.pallas_call(
            functools.partial(h_kernel, n_col),
            grid=(count,),
            in_specs=[
                SMEM,
                whole((tile, width)),
                pl.BlockSpec((tile, width), lambda t: (t + first, 0)),
            ],
            out_specs=whole((n_col, count, strip, tile)),
            out_shape=jax.ShapeDtypeStruct((n_col, count, strip, tile), BF16),
            compiler_params=params(),
            cost_estimate=cost(tile, tile),
        )(place, w, cot)

    def update(first, count, previous):
        return pl.pallas_call(
            functools.partial(update_kernel, slabs, tile),
            grid=(count,),
            in_specs=[
                pl.BlockSpec((tile, tile), lambda t: (0, t + first)),
                whole((tile, width)),
                pl.BlockSpec((mixed, LANES), lambda t: (t + first, 0)),
            ]
            + [ANY] * len(previous),
            out_specs=pl.BlockSpec((mixed, LANES), lambda t: (t + first, 0)),
            out_shape=jax.ShapeDtypeStruct((tiles * mixed, LANES), BF16),
            scratch_shapes=[pltpu.VMEM((mixed, LANES), F32)],
            input_output_aliases={3: 0} if previous else {},
            compiler_params=params(),
            cost_estimate=cost(2 * count * tile * width * tile, 4 * count * tile * width),
        )(panel_all, w, mixed_rows(slab), *previous)

    def halve(value, exchange, bit):
        half = value.shape[0] // 2
        return value[:half].astype(F32) + exchange(value[half:], bit).astype(F32)

    def sum_all(values):
        values = [v.astype(F32) for v in values]
        while len(values) > 1:
            values = [values[i] + values[i + 1] for i in range(0, len(values), 2)]
        return values[0]

    def row_sum(value, bits):
        steps = [sum(b for k, b in enumerate(bits) if (q >> k) & 1) for q in range(1 << len(bits))]
        return sum_all([value] + [permute_row(value, step) for step in steps[1:]])

    col_bits, row_bits = list(reversed(bits_of(n_col))), list(reversed(bits_of(n_row)))
    half = tiles // 2
    some = tiles * 3 // 8
    e_part = halve(e_part, permute_row, 1).astype(BF16)
    gi = sum_all([gi[0]] + [permute_col(gi[q], q) for q in range(1, n_col)]).astype(BF16)
    h_low = h_part(0, half)
    e_part, gi, h_low, w = lax.optimization_barrier((e_part, gi, h_low, w))

    gi = row_sum(gi, row_bits[:1]).astype(BF16)
    h_low = halve(h_low, permute_col, 1).astype(BF16)
    h_high = h_part(half, tiles - half)
    e_part, gi, h_low, h_high, w = lax.optimization_barrier((e_part, gi, h_low, h_high, w))

    for bit in col_bits[1:]:
        e_part = halve(e_part, permute_row, bit).astype(BF16)
    h_high = halve(h_high, permute_col, 1).astype(BF16)
    gi = row_sum(gi, row_bits[1:2])
    for bit in col_bits[1:]:
        h_low = halve(h_low.astype(BF16), permute_col, bit)
    updated = update(0, some, [])
    e_part, gi, h_high, updated, w = lax.optimization_barrier((e_part, gi, h_high, updated, w))

    for bit in col_bits[1:]:
        h_high = halve(h_high.astype(BF16), permute_col, bit)
    e_own = sum_all([transpose(e_part[m], m, back=True) for m in range(groups)])
    for bit in row_bits[2:]:
        gi = row_sum(gi.astype(BF16), [bit])
    updated = update(some, tiles - some, [updated])
    h_low, h_high, e_own, gi, updated = lax.optimization_barrier((h_low, h_high, e_own, gi, updated))
    h = jnp.concatenate([h_low[0], h_high[0]], 0)
    grad_panel = jnp.concatenate([h[:slots] + e_own, h[slots:]], 0)
    updated = updated.reshape(tiles, tile, tile // LANES, slabs, LANES).transpose(0, 1, 3, 2, 4)
    return (
        updated.reshape(slab.shape),
        grad_panel.transpose(0, 2, 1).reshape(panel.shape),
        gi.T,
    )


def solution(mesh):
    in_specs = (
        P(None, "row", None, "col"),
        P(None, "row", None, None, "col", None),
        P(None, "row", None, None, "col", None),
        P(),
    )
    out_specs = (
        P(None, "row", None, None, "col", None),
        P(None, "row", None, "col"),
        P(None, "col"),
    )
    return jax.shard_map(
        per_device, mesh=mesh, in_specs=in_specs, out_specs=out_specs, check_vma=False
    )
```

profile of v0, /device:TPU:0, one launch (start us, length us, event | category | flops | bytes accessed | tf_op | source)
XLA Modules:
  0.0 60.4 jit_solution(6165304653439372054)
XLA Ops:
  0.6 1.1 %fusion.2.refs_0_ = bf16[8,64,256]{2,1,0:T(8,128)(2,1)S(1)} fusion(f32[8,1,256,64]{2,3,1,0:T(8,128)} %param.4), kind=kLoop, calls=%fused_computation.8 | loop fusion | flops 131072 | bytes 786432 | tf_op jit(solution)/shard_map/convert_element_type | solution.py:200
  1.7 3.1 %collective-permute-start = (bf16[2,64,256]{2,1,0:T(8,128)(2,1)S(1)}, bf16[2,64,256]{2,1,0:T(8,128)(2,1)S(1)}, u32[]{:S(2)}, u32[]{:S(2)}) collective-permute-start(bf16[2,64,256]{2,1,0:T(8,128)(2,1)S(1)} %slice.89), channel_id=1, source_target_pairs={{0,8},{1,12},{2,0},{3,4},{4,9},{5,13},{6,1},{7,5},{8,10},{9,14},{1... | collective-permute-start | bytes 196616 | tf_op jit(solution)/shard_map/ppermute | solution.py:198
  4.8 3.5 %collective-permute-start.1 = (bf16[2,64,256]{2,1,0:T(8,128)(2,1)S(1)}, bf16[2,64,256]{2,1,0:T(8,128)(2,1)S(1)}, u32[]{:S(2)}, u32[]{:S(2)}) collective-permute-start(bf16[2,64,256]{2,1,0:T(8,128)(2,1)S(1)} %slice.89), channel_id=1, source_target_pairs={{0,24},{1,28},{2,16},{3,20},{4,25},{5,29},{6,17},{7,21},{8,26},{9,... | collective-permute-start | bytes 196616 | tf_op jit(solution)/shard_map/ppermute | solution.py:198
  8.3 0.5 collective-permute-start.4
  8.8 6.0 %shard_map.67 = (bf16[2048,1024]{1,0:T(8,128)(2,1)}, bf16[2,256,256]{2,1,0:T(8,128)(2,1)}) custom-call(f32[256,256]{1,0:T(8,128)} %refs_3_.1, bf16[16384,128]{1,0:T(8,128)(2,1)} %bitcast.54), custom_call_target="tpu_custom_call" | custom-call | bytes 8388608 | tf_op jit(solution)/shard_map/pallas_call | solution.py:204
  15.2 0.5 collective-permute-start.2
  15.6 5.3 %collective-permute-done.2 = bf16[2,2,64,256]{3,2,1,0:T(8,128)(2,1)S(1)} collective-permute-done((bf16[2,2,64,256]{3,2,1,0:T(8,128)(2,1)S(1)}, bf16[2,2,64,256]{3,2,1,0:T(8,128)(2,1)S(1)}, u32[]{:S(2)}, u32[]{:S(2)}) %collective-permute-start.2) | collective-permute-done | bytes 131104 | tf_op jit(solution)/shard_map/ppermute | solution.py:183
  21.1 2.2 %collective-permute-start.7 = (bf16[4,2,64,256]{3,2,1,0:T(8,128)(2,1)S(1)}, bf16[4,2,64,256]{3,2,1,0:T(8,128)(2,1)S(1)}, u32[]{:S(2)}, u32[]{:S(2)}) collective-permute-start(bf16[4,2,64,256]{3,2,1,0:T(8,128)(2,1)S(1)} %pad_maximum_fusion.1.refs_0_), channel_id=1, source_target_pairs={{0,4},{4,0},{8,12},{12,8},{16,20},{20,16},{24,28},{28,24},{1,5},{5... | collective-permute-start | bytes 786440 | tf_op jit(solution)/shard_map/ppermute | solution.py:183
  23.4 1.1 %copy-done.3 = bf16[2,256,256]{2,1,0:T(8,128)(2,1)S(1)} copy-done((bf16[2,256,256]{2,1,0:T(8,128)(2,1)S(1)}, bf16[2,256,256]{2,1,0:T(8,128)(2,1)}, u32[]{:S(2)}) %copy-start.3) | copy-done | bytes 262168
  24.5 4.1 %shard_map.68 = (bf16[4,256,256]{2,1,0:T(8,128)(2,1)S(1)}, bf16[8,2,64,256]{3,2,1,0:T(8,128)(2,1)S(1)}, bf16[256,2048]{1,0:T(8,128)(2,1)S(1)}) custom-call(s32[2]{0:T(128)S(1)} %pad_add_fusion.place_ref, bf16[8,64,256]{2,1,0:T(8,128)(2,1)S(1)} %fusion.2.refs_0_, bf16[8,64,256]{2,1,0:T(8,128)(2,1)S(1)} %collective-permute-done.3.refs_1_, ...), custom_call_target="tpu_custom_call" | custom-call | flops 1073741824 | bytes 5242880 | tf_op jit(solution)/shard_map/pallas_call | solution.py:239
  28.6 1.3 %collective-permute-start.6 = (bf16[4,2,64,256]{3,2,1,0:T(8,128)(2,1)S(1)}, bf16[4,2,64,256]{3,2,1,0:T(8,128)(2,1)S(1)}, u32[]{:S(2)}, u32[]{:S(2)}) collective-permute-start(bf16[4,2,64,256]{3,2,1,0:T(8,128)(2,1)S(1)} %slice.69), channel_id=1, source_target_pairs={{0,4},{4,0},{8,12},{12,8},{16,20},{20,16},{24,28},{28,24},{1,5},{5... | collective-permute-start | bytes 786440 | tf_op jit(solution)/shard_map/ppermute | solution.py:183
  30.2 1.7 %shard_map.69 = (bf16[256,1024]{1,0:T(8,128)(2,1)S(1)}, bf16[4,64,256]{2,1,0:T(8,128)(2,1)S(1)}) custom-call(s32[2]{0:T(128)S(1)} %pad_add_fusion.place_ref, bf16[4,2,64,256]{3,2,1,0:T(8,128)(2,1)S(1)} %pad_maximum_fusion.1.refs_0_, bf16[4,2,64,256]{3,2,1,0:T(8,128)(2,1)S(1)} %collective-permute-done.7.refs_1_, bf16[2,256,256]{2,1,0:T(8,128)(2,1)S(1)} %copy-done.3, ...), custom_call_target="tpu_custom_call" | custom-call | flops 256 | bytes 256 | tf_op jit(solution)/shard_map/pallas_call | solution.py:263
  31.9 1.0 %collective-permute-start.10 = (bf16[64,256]{1,0:T(8,128)(2,1)S(1)}, bf16[64,256]{1,0:T(8,128)(2,1)S(1)}, u32[]{:S(2)}, u32[]{:S(2)}) collective-permute-start(bf16[64,256]{1,0:T(8,128)(2,1)S(1)} %get-tuple-element.77), channel_id=1, source_target_pairs={{0,3},{1,2},{2,1},{3,0},{4,7},{5,6},{6,5},{7,4},{8,11},{9,10},{10,... | collective-permute-start | bytes 98312 | tf_op jit(solution)/shard_map/ppermute | solution.py:186
  32.9 0.7 %collective-permute-start.8 = (bf16[64,256]{1,0:T(8,128)(2,1)S(1)}, bf16[64,256]{1,0:T(8,128)(2,1)S(1)}, u32[]{:S(2)}, u32[]{:S(2)}) collective-permute-start(bf16[64,256]{1,0:T(8,128)(2,1)S(1)} %get-tuple-element.76), channel_id=1, source_target_pairs={{0,1},{1,0},{2,3},{3,2},{4,5},{5,4},{6,7},{7,6},{8,9},{9,8},{10,11... | collective-permute-start | bytes 98312 | tf_op jit(solution)/shard_map/ppermute | solution.py:186
  33.6 0.5 collective-permute-start.9
  34.1 2.0 %shard_map.70 = bf16[4,4,64,256]{3,2,1,0:T(8,128)(2,1)S(1)} custom-call(s32[2]{0:T(128)S(1)} %pad_add_fusion.place_ref, bf16[256,1024]{1,0:T(8,128)(2,1)S(1)} %get-tuple-element.64.w_ref, bf16[2048,1024]{1,0:T(8,128)(2,1)S(1)} %copy-done), custom_call_target="tpu_custom_call" | custom-call | flops 256 | bytes 256 | tf_op jit(solution)/shard_map/pallas_call | solution.py:277
  36.1 1.4 %collective-permute-done.9 = bf16[64,256]{1,0:T(8,128)(2,1)S(1)} collective-permute-done((bf16[64,256]{1,0:T(8,128)(2,1)S(1)}, bf16[64,256]{1,0:T(8,128)(2,1)S(1)}, u32[]{:S(2)}, u32[]{:S(2)}) %collective-permute-start.9) | collective-permute-done | bytes 32800 | tf_op jit(solution)/shard_map/ppermute | solution.py:186
  37.7 1.8 %collective-permute-start.11 = (bf16[64,256]{1,0:T(8,128)(2,1)S(1)}, bf16[64,256]{1,0:T(8,128)(2,1)S(1)}, u32[]{:S(2)}, u32[]{:S(2)}) collective-permute-start(bf16[64,256]{1,0:T(8,128)(2,1)S(1)} %fusion.4), channel_id=1, source_target_pairs={{0,4},{4,0},{8,12},{12,8},{16,20},{20,16},{24,28},{28,24},{1,5},{5... | collective-permute-start | bytes 98312 | tf_op jit(solution)/shard_map/ppermute | solution.py:183
  39.5 1.9 %shard_map.71 = bf16[4,4,64,256]{3,2,1,0:T(8,128)(2,1)S(1)} custom-call(s32[2]{0:T(128)S(1)} %pad_add_fusion.place_ref, bf16[256,1024]{1,0:T(8,128)(2,1)S(1)} %get-tuple-element.64.w_ref, bf16[2048,1024]{1,0:T(8,128)(2,1)S(1)} %copy-done), custom_call_target="tpu_custom_call" | custom-call | flops 256 | bytes 256 | tf_op jit(solution)/shard_map/pallas_call | solution.py:277
  41.9 0.5 collective-permute-start.15
  42.4 1.6 %collective-permute-start.14 = (bf16[2,2,64,256]{3,2,1,0:T(8,128)(2,1)S(1)}, bf16[2,2,64,256]{3,2,1,0:T(8,128)(2,1)S(1)}, u32[]{:S(2)}, u32[]{:S(2)}) collective-permute-start(bf16[2,2,64,256]{3,2,1,0:T(8,128)(2,1)S(1)} %slice.79), channel_id=1, source_target_pairs={{0,8},{4,12},{8,0},{12,4},{16,24},{20,28},{24,16},{28,20},{1,9},{5... | collective-permute-start | bytes 393224 | tf_op jit(solution)/shard_map/ppermute | solution.py:183
  44.1 1.1 %collective-permute-start.13 = (bf16[1,4,64,256]{3,2,1,0:T(8,128)(2,1)S(1)}, bf16[1,4,64,256]{3,2,1,0:T(8,128)(2,1)S(1)}, u32[]{:S(2)}, u32[]{:S(2)}) collective-permute-start(bf16[1,4,64,256]{3,2,1,0:T(8,128)(2,1)S(1)} %slice.77), channel_id=1, source_target_pairs={{0,2},{1,3},{2,0},{3,1},{4,6},{5,7},{6,4},{7,5},{8,10},{9,11},{10,... | collective-permute-start | bytes 393224 | tf_op jit(solution)/shard_map/ppermute | solution.py:186
  45.2 2.5 %shard_map.72.refs_0_ = bf16[16384,128]{1,0:T(8,128)(2,1)} custom-call(bf16[256,2048]{1,0:T(8,128)(2,1)S(1)} %get-tuple-element.59.pt_ref, bf16[256,1024]{1,0:T(8,128)(2,1)S(1)} %get-tuple-element.64.w_ref, bf16[16384,128]{1,0:T(8,128)(2,1)S(1)} %bitcast.51), custom_call_target="tpu_custom_call" | custom-call | flops 402653184 | bytes 3145728 | tf_op jit(solution)/shard_map/pallas_call | solution.py:292
  47.7 0.8 %collective-permute-done.14 = bf16[2,2,64,256]{3,2,1,0:T(8,128)(2,1)S(1)} collective-permute-done((bf16[2,2,64,256]{3,2,1,0:T(8,128)(2,1)S(1)}, bf16[2,2,64,256]{3,2,1,0:T(8,128)(2,1)S(1)}, u32[]{:S(2)}, u32[]{:S(2)}) %collective-permute-start.14) | collective-permute-done | bytes 131104 | tf_op jit(solution)/shard_map/ppermute | solution.py:183
  48.5 0.9 %collective-permute-done.13 = bf16[1,4,64,256]{3,2,1,0:T(8,128)(2,1)S(1)} collective-permute-done((bf16[1,4,64,256]{3,2,1,0:T(8,128)(2,1)S(1)}, bf16[1,4,64,256]{3,2,1,0:T(8,128)(2,1)S(1)}, u32[]{:S(2)}, u32[]{:S(2)}) %collective-permute-start.13) | collective-permute-done | bytes 131104 | tf_op jit(solution)/shard_map/ppermute | solution.py:186
  49.6 1.1 %collective-permute-start.18 = (bf16[2,64,256]{2,1,0:T(8,128)(2,1)S(1)}, bf16[2,64,256]{2,1,0:T(8,128)(2,1)S(1)}, u32[]{:S(2)}, u32[]{:S(2)}) collective-permute-start(bf16[2,64,256]{2,1,0:T(8,128)(2,1)S(1)} %get-tuple-element.74), channel_id=1, source_target_pairs={{8,0},{12,1},{0,2},{4,3},{9,4},{13,5},{1,6},{5,7},{10,8},{14,9},{2... | collective-permute-start | bytes 196616 | tf_op jit(solution)/shard_map/ppermute | solution.py:198
  50.7 2.8 %collective-permute-start.19 = (bf16[2,64,256]{2,1,0:T(8,128)(2,1)S(1)}, bf16[2,64,256]{2,1,0:T(8,128)(2,1)S(1)}, u32[]{:S(2)}, u32[]{:S(2)}) collective-permute-start(bf16[2,64,256]{2,1,0:T(8,128)(2,1)S(1)} %get-tuple-element.75), channel_id=1, source_target_pairs={{24,0},{28,1},{16,2},{20,3},{25,4},{29,5},{17,6},{21,7},{26,8},{30... | collective-permute-start | bytes 196616 | tf_op jit(solution)/shard_map/ppermute | solution.py:198
  53.5 1.0 %collective-permute-start.17 = (bf16[1,4,64,256]{3,2,1,0:T(8,128)(2,1)S(1)}, bf16[1,4,64,256]{3,2,1,0:T(8,128)(2,1)S(1)}, u32[]{:S(2)}, u32[]{:S(2)}) collective-permute-start(bf16[1,4,64,256]{3,2,1,0:T(8,128)(2,1)S(1)} %slice.83), channel_id=1, source_target_pairs={{0,2},{1,3},{2,0},{3,1},{4,6},{5,7},{6,4},{7,5},{8,10},{9,11},{10,... | collective-permute-start | bytes 393224 | tf_op jit(solution)/shard_map/ppermute | solution.py:186
  54.6 3.8 %shard_map.73 = bf16[16384,128]{1,0:T(8,128)(2,1)} custom-call(bf16[256,2048]{1,0:T(8,128)(2,1)S(1)} %get-tuple-element.59.pt_ref, bf16[256,1024]{1,0:T(8,128)(2,1)S(1)} %get-tuple-element.64.w_ref, bf16[16384,128]{1,0:T(8,128)(2,1)S(1)} %bitcast.52, bf16[16384,128]{1,0:T(8,128)(2,1)} %shard_map.72.refs_0_), custom_call_target="tpu_custom_call", output_to_operand_aliasing={{}: (3, {})} | custom-call | flops 671088640 | bytes 5242880 | tf_op jit(solution)/shard_map/pallas_call | solution.py:292
  58.4 0.6 %convert_add_fusion.4 = f32[64,256]{1,0:T(8,128)} fusion(bf16[64,256]{1,0:T(8,128)(2,1)S(1)} %collective-permute-done.20, bf16[64,256]{1,0:T(8,128)(2,1)S(1)} %convert_add_fusion.5), kind=kLoop, calls=%fused_computation.19 | loop fusion | flops 49152 | bytes 131072 | tf_op jit(solution)/shard_map/add | solution.py:316
  59.0 0.5 collective-permute-done.17
  59.5 0.8 %fusion.1 = f32[8,1,256,64]{2,3,1,0:T(8,128)} fusion(f32[4,64,256]{2,1,0:T(8,128)S(1)} %bitcast.56, f32[4,64,256]{2,1,0:T(8,128)S(1)} %bitcast.55, f32[2,64,256]{2,1,0:T(8,128)S(1)} %bitcast_add_fusion), kind=kLoop, calls=%fused_computation.2 | loop fusion | flops 524288 | bytes 1179648
  (51 shorter events, 1.6 us)
Async XLA Ops:
  1.7 13.2 %collective-permute-start = (bf16[2,64,256]{2,1,0:T(8,128)(2,1)S(1)}, bf16[2,64,256]{2,1,0:T(8,128)(2,1)S(1)}, u32[]{:S(2)}, u32[]{:S(2)}) collective-permute-start(bf16[2,64,256]{2,1,0:T(8,128)(2,1)S(1)} %slice.89), channel_id=1, source_target_pairs={{0,8},{1,12},{2,0},{3,4},{4,9},{5,13},{6,1},{7,5},{8,10},{9,14},{1... | collective-permute-start | bytes 196616 | tf_op jit(solution)/shard_map/ppermute | solution.py:198
  4.8 10.1 %collective-permute-start.1 = (bf16[2,64,256]{2,1,0:T(8,128)(2,1)S(1)}, bf16[2,64,256]{2,1,0:T(8,128)(2,1)S(1)}, u32[]{:S(2)}, u32[]{:S(2)}) collective-permute-start(bf16[2,64,256]{2,1,0:T(8,128)(2,1)S(1)} %slice.89), channel_id=1, source_target_pairs={{0,24},{1,28},{2,16},{3,20},{4,25},{5,29},{6,17},{7,21},{8,26},{9,... | collective-permute-start | bytes 196616 | tf_op jit(solution)/shard_map/ppermute | solution.py:198
  8.3 12.7 %collective-permute-start.4 = (bf16[8,64,256]{2,1,0:T(8,128)(2,1)S(1)}, bf16[8,64,256]{2,1,0:T(8,128)(2,1)S(1)}, u32[]{:S(2)}, u32[]{:S(2)}) collective-permute-start(bf16[8,64,256]{2,1,0:T(8,128)(2,1)S(1)} %fusion.2.refs_0_), channel_id=1, source_target_pairs={{0,2},{1,3},{2,0},{3,1},{4,6},{5,7},{6,4},{7,5},{8,10},{9,11},{10,... | collective-permute-start | bytes 786440 | tf_op jit(solution)/shard_map/ppermute | solution.py:186
  14.9 15.3 %copy-start.2 = (f32[256,256]{1,0:T(8,128)S(1)}, f32[256,256]{1,0:T(8,128)}, u32[]{:S(2)}) copy-start(f32[256,256]{1,0:T(8,128)} %refs_3_.1) | copy-start | bytes 786436
  14.9 6.1 %collective-permute-start.3 = (bf16[8,64,256]{2,1,0:T(8,128)(2,1)S(1)}, bf16[8,64,256]{2,1,0:T(8,128)(2,1)S(1)}, u32[]{:S(2)}, u32[]{:S(2)}) collective-permute-start(bf16[8,64,256]{2,1,0:T(8,128)(2,1)S(1)} %fusion.2.refs_0_), channel_id=1, source_target_pairs={{0,1},{1,0},{2,3},{3,2},{4,5},{5,4},{6,7},{7,6},{8,9},{9,8},{10,11... | collective-permute-start | bytes 786440 | tf_op jit(solution)/shard_map/ppermute | solution.py:186
  15.2 5.8 %collective-permute-start.2 = (bf16[2,2,64,256]{3,2,1,0:T(8,128)(2,1)S(1)}, bf16[2,2,64,256]{3,2,1,0:T(8,128)(2,1)S(1)}, u32[]{:S(2)}, u32[]{:S(2)}) collective-permute-start(bf16[2,2,64,256]{3,2,1,0:T(8,128)(2,1)S(1)} %pad_maximum_fusion.2), channel_id=1, source_target_pairs={{0,8},{4,12},{8,0},{12,4},{16,24},{20,28},{24,16},{28,20},{1,9},{5... | collective-permute-start | bytes 393224 | tf_op jit(solution)/shard_map/ppermute | solution.py:183
  21.0 2.4 %collective-permute-start.5 = (bf16[8,64,256]{2,1,0:T(8,128)(2,1)S(1)}, bf16[8,64,256]{2,1,0:T(8,128)(2,1)S(1)}, u32[]{:S(2)}, u32[]{:S(2)}) collective-permute-start(bf16[8,64,256]{2,1,0:T(8,128)(2,1)S(1)} %collective-permute-done.4.refs_2_), channel_id=1, source_target_pairs={{0,1},{1,0},{2,3},{3,2},{4,5},{5,4},{6,7},{7,6},{8,9},{9,8},{10,11... | collective-permute-start | bytes 786440 | tf_op jit(solution)/shard_map/ppermute | solution.py:186
  21.1 9.1 %collective-permute-start.7 = (bf16[4,2,64,256]{3,2,1,0:T(8,128)(2,1)S(1)}, bf16[4,2,64,256]{3,2,1,0:T(8,128)(2,1)S(1)}, u32[]{:S(2)}, u32[]{:S(2)}) collective-permute-start(bf16[4,2,64,256]{3,2,1,0:T(8,128)(2,1)S(1)} %pad_maximum_fusion.1.refs_0_), channel_id=1, source_target_pairs={{0,4},{4,0},{8,12},{12,8},{16,20},{20,16},{24,28},{28,24},{1,5},{5... | collective-permute-start | bytes 786440 | tf_op jit(solution)/shard_map/ppermute | solution.py:183
  23.3 10.8 %copy-start = (bf16[2048,1024]{1,0:T(8,128)(2,1)S(1)}, bf16[2048,1024]{1,0:T(8,128)(2,1)}, u32[]{:S(2)}) copy-start(bf16[2048,1024]{1,0:T(8,128)(2,1)} %get-tuple-element.45.refs_5_.g_ref) | copy-start | bytes 12582916
  23.4 1.1 %copy-start.3 = (bf16[2,256,256]{2,1,0:T(8,128)(2,1)S(1)}, bf16[2,256,256]{2,1,0:T(8,128)(2,1)}, u32[]{:S(2)}) copy-start(bf16[2,256,256]{2,1,0:T(8,128)(2,1)} %get-tuple-element.44.refs_4_.refs_2_) | copy-start | bytes 786436
  28.6 8.9 %collective-permute-start.6 = (bf16[4,2,64,256]{3,2,1,0:T(8,128)(2,1)S(1)}, bf16[4,2,64,256]{3,2,1,0:T(8,128)(2,1)S(1)}, u32[]{:S(2)}, u32[]{:S(2)}) collective-permute-start(bf16[4,2,64,256]{3,2,1,0:T(8,128)(2,1)S(1)} %slice.69), channel_id=1, source_target_pairs={{0,4},{4,0},{8,12},{12,8},{16,20},{20,16},{24,28},{28,24},{1,5},{5... | collective-permute-start | bytes 786440 | tf_op jit(solution)/shard_map/ppermute | solution.py:183
  31.9 4.2 %collective-permute-start.10 = (bf16[64,256]{1,0:T(8,128)(2,1)S(1)}, bf16[64,256]{1,0:T(8,128)(2,1)S(1)}, u32[]{:S(2)}, u32[]{:S(2)}) collective-permute-start(bf16[64,256]{1,0:T(8,128)(2,1)S(1)} %get-tuple-element.77), channel_id=1, source_target_pairs={{0,3},{1,2},{2,1},{3,0},{4,7},{5,6},{6,5},{7,4},{8,11},{9,10},{10,... | collective-permute-start | bytes 98312 | tf_op jit(solution)/shard_map/ppermute | solution.py:186
  32.9 3.2 %collective-permute-start.8 = (bf16[64,256]{1,0:T(8,128)(2,1)S(1)}, bf16[64,256]{1,0:T(8,128)(2,1)S(1)}, u32[]{:S(2)}, u32[]{:S(2)}) collective-permute-start(bf16[64,256]{1,0:T(8,128)(2,1)S(1)} %get-tuple-element.76), channel_id=1, source_target_pairs={{0,1},{1,0},{2,3},{3,2},{4,5},{5,4},{6,7},{7,6},{8,9},{9,8},{10,11... | collective-permute-start | bytes 98312 | tf_op jit(solution)/shard_map/ppermute | solution.py:186
  33.6 3.9 %collective-permute-start.9 = (bf16[64,256]{1,0:T(8,128)(2,1)S(1)}, bf16[64,256]{1,0:T(8,128)(2,1)S(1)}, u32[]{:S(2)}, u32[]{:S(2)}) collective-permute-start(bf16[64,256]{1,0:T(8,128)(2,1)S(1)} %get-tuple-element.78), channel_id=1, source_target_pairs={{0,2},{1,3},{2,0},{3,1},{4,6},{5,7},{6,4},{7,5},{8,10},{9,11},{10,... | collective-permute-start | bytes 98312 | tf_op jit(solution)/shard_map/ppermute | solution.py:186
  37.5 7.7 %copy-start.1 = (bf16[8,1,256,4,1,256]{5,3,4,2,1,0:T(4,128)(2,1)S(1)}, bf16[8,1,256,4,1,256]{5,3,4,2,1,0:T(4,128)(2,1)}, u32[]{:S(2)}) copy-start(bf16[8,1,256,4,1,256]{5,3,4,2,1,0:T(4,128)(2,1)} %param.5) | copy-start | bytes 12582916
  37.6 4.1 %collective-permute-start.12 = (bf16[2,4,64,256]{3,2,1,0:T(8,128)(2,1)S(1)}, bf16[2,4,64,256]{3,2,1,0:T(8,128)(2,1)S(1)}, u32[]{:S(2)}, u32[]{:S(2)}) collective-permute-start(bf16[2,4,64,256]{3,2,1,0:T(8,128)(2,1)S(1)} %slice.75), channel_id=1, source_target_pairs={{0,1},{1,0},{2,3},{3,2},{4,5},{5,4},{6,7},{7,6},{8,9},{9,8},{10,11... | collective-permute-start | bytes 786440 | tf_op jit(solution)/shard_map/ppermute | solution.py:186
  37.7 4.0 %collective-permute-start.11 = (bf16[64,256]{1,0:T(8,128)(2,1)S(1)}, bf16[64,256]{1,0:T(8,128)(2,1)S(1)}, u32[]{:S(2)}, u32[]{:S(2)}) collective-permute-start(bf16[64,256]{1,0:T(8,128)(2,1)S(1)} %fusion.4), channel_id=1, source_target_pairs={{0,4},{4,0},{8,12},{12,8},{16,20},{20,16},{24,28},{28,24},{1,5},{5... | collective-permute-start | bytes 98312 | tf_op jit(solution)/shard_map/ppermute | solution.py:183
  41.8 7.7 %collective-permute-start.16 = (bf16[2,4,64,256]{3,2,1,0:T(8,128)(2,1)S(1)}, bf16[2,4,64,256]{3,2,1,0:T(8,128)(2,1)S(1)}, u32[]{:S(2)}, u32[]{:S(2)}) collective-permute-start(bf16[2,4,64,256]{3,2,1,0:T(8,128)(2,1)S(1)} %slice.81), channel_id=1, source_target_pairs={{0,1},{1,0},{2,3},{3,2},{4,5},{5,4},{6,7},{7,6},{8,9},{9,8},{10,11... | collective-permute-start | bytes 786440 | tf_op jit(solution)/shard_map/ppermute | solution.py:186
  41.9 5.8 %collective-permute-start.15 = (bf16[64,256]{1,0:T(8,128)(2,1)S(1)}, bf16[64,256]{1,0:T(8,128)(2,1)S(1)}, u32[]{:S(2)}, u32[]{:S(2)}) collective-permute-start(bf16[64,256]{1,0:T(8,128)(2,1)S(1)} %add_convert_fusion.4), channel_id=1, source_target_pairs={{0,8},{4,12},{8,0},{12,4},{16,24},{20,28},{24,16},{28,20},{1,9},{5... | collective-permute-start | bytes 98312 | tf_op jit(solution)/shard_map/ppermute | solution.py:183
  42.4 6.1 %collective-permute-start.14 = (bf16[2,2,64,256]{3,2,1,0:T(8,128)(2,1)S(1)}, bf16[2,2,64,256]{3,2,1,0:T(8,128)(2,1)S(1)}, u32[]{:S(2)}, u32[]{:S(2)}) collective-permute-start(bf16[2,2,64,256]{3,2,1,0:T(8,128)(2,1)S(1)} %slice.79), channel_id=1, source_target_pairs={{0,8},{4,12},{8,0},{12,4},{16,24},{20,28},{24,16},{28,20},{1,9},{5... | collective-permute-start | bytes 393224 | tf_op jit(solution)/shard_map/ppermute | solution.py:183
  44.1 5.4 %collective-permute-start.13 = (bf16[1,4,64,256]{3,2,1,0:T(8,128)(2,1)S(1)}, bf16[1,4,64,256]{3,2,1,0:T(8,128)(2,1)S(1)}, u32[]{:S(2)}, u32[]{:S(2)}) collective-permute-start(bf16[1,4,64,256]{3,2,1,0:T(8,128)(2,1)S(1)} %slice.77), channel_id=1, source_target_pairs={{0,2},{1,3},{2,0},{3,1},{4,6},{5,7},{6,4},{7,5},{8,10},{9,11},{10,... | collective-permute-start | bytes 393224 | tf_op jit(solution)/shard_map/ppermute | solution.py:186
  49.5 8.8 %collective-permute-start.20 = (bf16[64,256]{1,0:T(8,128)(2,1)S(1)}, bf16[64,256]{1,0:T(8,128)(2,1)S(1)}, u32[]{:S(2)}, u32[]{:S(2)}) collective-permute-start(bf16[64,256]{1,0:T(8,128)(2,1)S(1)} %convert_add_fusion.5), channel_id=1, source_target_pairs={{0,16},{4,20},{8,24},{12,28},{16,0},{20,4},{24,8},{28,12},{1,17},{... | collective-permute-start | bytes 98312 | tf_op jit(solution)/shard_map/ppermute | solution.py:183
  49.6 9.4 %collective-permute-start.18 = (bf16[2,64,256]{2,1,0:T(8,128)(2,1)S(1)}, bf16[2,64,256]{2,1,0:T(8,128)(2,1)S(1)}, u32[]{:S(2)}, u32[]{:S(2)}) collective-permute-start(bf16[2,64,256]{2,1,0:T(8,128)(2,1)S(1)} %get-tuple-element.74), channel_id=1, source_target_pairs={{8,0},{12,1},{0,2},{4,3},{9,4},{13,5},{1,6},{5,7},{10,8},{14,9},{2... | collective-permute-start | bytes 196616 | tf_op jit(solution)/shard_map/ppermute | solution.py:198
  50.7 8.3 %collective-permute-start.19 = (bf16[2,64,256]{2,1,0:T(8,128)(2,1)S(1)}, bf16[2,64,256]{2,1,0:T(8,128)(2,1)S(1)}, u32[]{:S(2)}, u32[]{:S(2)}) collective-permute-start(bf16[2,64,256]{2,1,0:T(8,128)(2,1)S(1)} %get-tuple-element.75), channel_id=1, source_target_pairs={{24,0},{28,1},{16,2},{20,3},{25,4},{29,5},{17,6},{21,7},{26,8},{30... | collective-permute-start | bytes 196616 | tf_op jit(solution)/shard_map/ppermute | solution.py:198
  53.5 5.9 %collective-permute-start.17 = (bf16[1,4,64,256]{3,2,1,0:T(8,128)(2,1)S(1)}, bf16[1,4,64,256]{3,2,1,0:T(8,128)(2,1)S(1)}, u32[]{:S(2)}, u32[]{:S(2)}) collective-permute-start(bf16[1,4,64,256]{3,2,1,0:T(8,128)(2,1)S(1)} %slice.83), channel_id=1, source_target_pairs={{0,2},{1,3},{2,0},{3,1},{4,6},{5,7},{6,4},{7,5},{8,10},{9,11},{10,... | collective-permute-start | bytes 393224 | tf_op jit(solution)/shard_map/ppermute | solution.py:186
where the time goes:
time: 60.6 us; the launch traced here: 60.4 us
  starting transfers between devices  23.9 us (39%)
  Pallas kernels  22 us (36%)
  waiting for transfers between devices  9.33 us (15%)
  other arithmetic  3.03 us (5%)
  local copies, waits for them, and re-layouts  1.23 us (2%)
  between operations  0.93 us (2%)
    ppermute x4, starting transfers between devices, transpose(): return lax.ppermute(value, BOTH, pairs)  10.5 us
    ppermute x7, starting transfers between devices, permute_row(): return lax.ppermute(value, 'row', [(i, i ^ bit) for i in range(n_row)])  8.04 us
    ppermute x7, waiting for transfers between devices, permute_row(): return lax.ppermute(value, 'row', [(i, i ^ bit) for i in range(n_row)])  6.57 us
    pallas_call x2, Pallas kernels, update(): pl.pallas_call(functools.partial(update_kernel, slabs, tile), grid=(count...  6.26 us
    pallas_call x1, Pallas kernels, per_device(): pl.pallas_call(functools.partial(unmix_kernel, slabs, tile), grid=(tiles,...  6.01 us
    ppermute x10, starting transfers between devices, permute_col(): return lax.ppermute(value, 'col', [(i, i ^ bit) for i in range(n_col)])  5.35 us
    pallas_call x1, Pallas kernels, per_device(): pl.pallas_call(functools.partial(q_kernel, n_row, n_col, groups), grid=(s...  4.13 us
    pallas_call x2, Pallas kernels, h_part(): pl.pallas_call(functools.partial(h_kernel, n_col), grid=(count,), in_spec...  3.9 us
  transfers between devices with their start and end apart: 21, of which 7 were waited for; matrix products, arithmetic and copies ran while one was open for 2% of the time, Pallas kernels for 36%

commit v1 on v0

--- a/solution.py
+++ b/solution.py
@@ -45,26 +45,31 @@
     return pl.CostEstimate(flops=flops, bytes_accessed=nbytes, transcendentals=0)
 
 
-def unmix_kernel(slabs, tile, inv_ref, x_ref, o_ref, m_ref, wide_ref, ins, outs, in_sems, out_sems):
+def unmix_kernel(slabs, tile, first, *refs):
+    if first:
+        x_ref, _, o_ref, wide_ref, ins, outs, in_sems, out_sems = refs
+    else:
+        inv_ref, x_ref, o_ref, m_ref, wide_ref, ins, outs, in_sems, out_sems = refs
     step, steps = pl.program_id(0), ins.shape[0]
     size = ins.shape[1]
 
     def copy_in(t):
-        at = pl.multiple_of(t * size, size)
+        at = pl.multiple_of((first + t) * size, size)
         return pltpu.make_async_copy(x_ref.at[pl.ds(at, size)], ins.at[t], in_sems.at[t])
 
     def copy_out(t):
-        at = pl.multiple_of(t * tile, tile)
+        at = pl.multiple_of((first + t) * tile, tile)
         return pltpu.make_async_copy(outs.at[t], o_ref.at[pl.ds(at, tile)], out_sems.at[t])
 
     @pl.when(step == 0)
     def _():
         for t in range(steps):
             copy_in(t).start()
-        mat = dot(inv_ref[...], inv_ref[...], ((0,), (0,)), lax.Precision.HIGHEST)
-        high = mat.astype(BF16)
-        m_ref[0] = high
-        m_ref[1] = (mat - high.astype(F32)).astype(BF16)
+        if not first:
+            mat = dot(inv_ref[...], inv_ref[...], ((0,), (0,)), lax.Precision.HIGHEST)
+            high = mat.astype(BF16)
+            m_ref[0] = high
+            m_ref[1] = (mat - high.astype(F32)).astype(BF16)
 
     copy_in(step).wait()
     halves = tile // LANES
@@ -82,7 +87,8 @@
 
 
 def q_kernel(n_row, n_col, groups, place_ref, *refs):
-    parts, (m_ref, g_ref, q_ref, e_ref, pt_ref, ins, sems) = refs[:n_col], refs[n_col:]
+    parts, (m_any, g_ref, q_ref, e_ref, pt_ref, ins, m_ref, sems) = refs[:n_col], refs[n_col:]
+    copy_m = pltpu.make_async_copy(m_any, m_ref, sems.at[ins.shape[0]])
     tiles, strip, tile = parts[0].shape
     s = pl.program_id(0)
     row, col = place_ref[0], place_ref[1]
@@ -96,6 +102,7 @@
     def _():
         for at in range(ins.shape[0]):
             copy_in(at).start()
+        copy_m.start()
         for q in range(n_col):
             at = pl.multiple_of((col ^ q) * strip, strip)
             for t in range(tiles):
@@ -106,29 +113,27 @@
 
     @pl.when(s == pl.num_programs(0) - 1)
     def _():
+        copy_m.wait()
         for at in range(q_ref.shape[0]):
             q_val = q_ref[at]
             e_val = -(dot(m_ref[0], q_val, ((1,), (0,))) + dot(m_ref[1], q_val, ((1,), (0,))))
             e_val = e_val.astype(BF16)
             slot, other = at // groups, group ^ (at % groups)
             for r in range(n_col):
-                place = reversed_bits(rho ^ r, n_col) * groups + other
-                e_ref[place, slot] = e_val[r * strip : (r + 1) * strip]
+                e_ref[rho ^ r, other, slot] = e_val[r * strip : (r + 1) * strip]
 
 
 def w_kernel(n_row, n_col, groups, place_ref, *refs):
-    tops, (m_ref, inv_ref, q_ref, w_ref, gi_ref, top_all) = refs[:2], refs[2:]
+    tops, (m_ref, inv_ref, q_ref, w_ref, gi_ref, top_all) = refs[:n_col], refs[n_col:]
     slots, strip, tile = tops[0].shape[1:]
-    half = tops[0].shape[0]
     slabs = slots * groups
     row, col = place_ref[0], place_ref[1]
     group, rho = row // n_col, (row % n_col) ^ (n_col // 2)
     for p in range(n_row):
         at = pl.multiple_of((rho ^ (p % n_col)) * strip, strip)
-        place = reversed_bits(p % n_col, n_col) * groups + p // n_col
         for slot in range(slots):
             s = slot * groups + (group ^ (p // n_col))
-            top_all[s, pl.ds(at, strip), :] = tops[place // half][place % half, slot]
+            top_all[s, pl.ds(at, strip), :] = tops[p % n_col][p // n_col, slot]
     z = jnp.zeros((tile, tile), F32)
     for s in range(slabs):
         top = top_all[s]
@@ -138,7 +143,7 @@
     z = z + z.T
     gi = -dot(z, inv_ref[...], ((1,), (1,)), lax.Precision.HIGHEST)
     for r in range(n_col):
-        gi_ref[col ^ r] = gi[r * strip : (r + 1) * strip].astype(BF16)
+        gi_ref[reversed_bits(col ^ r, n_col)] = gi[r * strip : (r + 1) * strip].astype(BF16)
 
 
 def h_kernel(n_col, place_ref, w_ref, g_ref, h_ref):
@@ -198,63 +203,67 @@
         return lax.ppermute(value, BOTH, pairs)
 
     own = panel.reshape(tiles, tile, strip).transpose(0, 2, 1).astype(BF16)
-    high, *lower = bits_of(n_col)
-    parts = {0: own, high: permute_col(own, high)}
-    tops = [transpose(own[:slots], m) for m in range(groups)]
-    cot, mat = pl.pallas_call(
-        functools.partial(unmix_kernel, slabs, tile),
-        grid=(tiles,),
-        in_specs=[whole((tile, tile)), ANY],
-        out_specs=[ANY, whole((2, tile, tile))],
-        out_shape=[
+    def unmix(first, count, *args):
+        outs = [ANY] if first else [ANY, whole((2, tile, tile))]
+        shapes = [
             jax.ShapeDtypeStruct((rows, width), BF16),
             jax.ShapeDtypeStruct((2, tile, tile), BF16),
-        ],
-        scratch_shapes=[
-            pltpu.VMEM((mixed, LANES), F32),
-            pltpu.VMEM((tiles, mixed, LANES), BF16),
-            pltpu.VMEM((tiles, tile, width), BF16),
-            pltpu.SemaphoreType.DMA((tiles,)),
-            pltpu.SemaphoreType.DMA((tiles,)),
-        ],
-        compiler_params=params(STREAMED),
-        cost_estimate=cost(0, 4 * rows * width),
-    )(inverse, mixed_rows(cotangent))
-
-    tops, own, mat = lax.optimization_barrier((tops, own, mat))
-
-    top = jnp.stack(tops)
-    for bit in bits_of(n_col)[:-1]:
-        top = jnp.concatenate([top, permute_row(top, bit)], 0)
+        ]
+        return pl.pallas_call(
+            functools.partial(unmix_kernel, slabs, tile, first),
+            grid=(count,),
+            in_specs=[ANY, ANY] if first else [whole((tile, tile)), ANY],
+            out_specs=outs,
+            out_shape=shapes[: len(outs)],
+            scratch_shapes=[
+                pltpu.VMEM((mixed, LANES), F32),
+                pltpu.VMEM((count, mixed, LANES), BF16),
+                pltpu.VMEM((count, tile, width), BF16),
+                pltpu.SemaphoreType.DMA((count,)),
+                pltpu.SemaphoreType.DMA((count,)),
+            ],
+            input_output_aliases={1: 0} if first else {},
+            compiler_params=params(STREAMED),
+            cost_estimate=cost(0, 4 * count * tile * width),
+        )(*args)
+
+    high, *lower = bits_of(n_col)
+    half = tiles // 2
+    parts = {0: own, high: permute_col(own, high)}
     if lower:
         parts[1] = permute_col(own, 1)
-    top, parts = lax.optimization_barrier((top, parts))
-
+    tops = [transpose(own[:slots], m) for m in range(groups)]
+    cot, mat = unmix(0, half, inverse, mixed_rows(cotangent))
+    tops, parts, mat = lax.optimization_barrier((tops, parts, mat))
+
+    top = jnp.stack(tops)
+    tops = [top] + [permute_row(top, q) for q in range(1, n_col)]
     for bit in lower:
         for q in range(0, n_col, 2 * bit):
             if q | bit not in parts:
                 parts[q | bit] = permute_col(parts[q], bit)
-    tops = [top, permute_row(top, 1)]
+    (cot,) = unmix(half, tiles - half, mixed_rows(cotangent), cot)
 
     q_sum, e_part, panel_all = pl.pallas_call(
         functools.partial(q_kernel, n_row, n_col, groups),
         grid=(slabs,),
         in_specs=[SMEM]
         + [whole((tiles, strip, tile))] * n_col
-        + [whole((2, tile, tile)), ANY],
+        + [ANY, ANY],
         out_specs=[
             whole((slabs, tile, tile)),
-            whole((n_row, slots, strip, tile)),
+            whole((n_col, groups, slots, strip, tile)),
             whole((tile, rows)),
         ],
         out_shape=[
             jax.ShapeDtypeStruct((slabs, tile, tile), BF16),
-            jax.ShapeDtypeStruct((n_row, slots, strip, tile), BF16),
+            jax.ShapeDtypeStruct((n_col, groups, slots, strip, tile), BF16),
             jax.ShapeDtypeStruct((tile, rows), BF16),
         ],
         scratch_shapes=[
             pltpu.VMEM((slabs, rows, tile), BF16),
-            pltpu.SemaphoreType.DMA((slabs,)),
+            pltpu.VMEM((2, tile, tile), BF16),
+            pltpu.SemaphoreType.DMA((slabs + 1,)),
         ],
         compiler_params=params(STREAMED - 10),
         cost_estimate=cost(2 * rows * width * tile, 2 * rows * (width + tile)),
@@ -262,7 +271,7 @@
 
     w, gi = pl.pallas_call(
         functools.partial(w_kernel, n_row, n_col, groups),
-        in_specs=[SMEM] + [VMEM] * 5,
+        in_specs=[SMEM] + [VMEM] * (n_col + 3),
         out_specs=[VMEM, VMEM],
         out_shape=[
             jax.ShapeDtypeStruct((tile, width), BF16),
@@ -285,7 +294,7 @@
             out_specs=whole((n_col, count, strip, tile)),
             out_shape=jax.ShapeDtypeStruct((n_col, count, strip, tile), BF16),
             compiler_params=params(),
-            cost_estimate=cost(tile, tile),
+            cost_estimate=cost(2 * count * tile * width * tile, 4 * count * tile * width),
         )(place, w, cot)
 
     def update(first, count, previous):
@@ -321,34 +330,32 @@
         return sum_all([value] + [permute_row(value, step) for step in steps[1:]])
 
     col_bits, row_bits = list(reversed(bits_of(n_col))), list(reversed(bits_of(n_row)))
-    half = tiles // 2
     some = tiles * 3 // 8
-    e_part = halve(e_part, permute_row, 1).astype(BF16)
-    gi = sum_all([gi[0]] + [permute_col(gi[q], q) for q in range(1, n_col)]).astype(BF16)
+    e_part = sum_all([e_part[0]] + [permute_row(e_part[q], q) for q in range(1, n_col)]).astype(BF16)
+    gi = halve(gi, permute_col, 1).astype(BF16)
     h_low = h_part(0, half)
     e_part, gi, h_low, w = lax.optimization_barrier((e_part, gi, h_low, w))
 
-    gi = row_sum(gi, row_bits[:1]).astype(BF16)
+    e_own = sum_all([transpose(e_part[m], m, back=True) for m in range(groups)])
+    for bit in col_bits[1:]:
+        gi = halve(gi, permute_col, bit).astype(BF16)
     h_low = halve(h_low, permute_col, 1).astype(BF16)
     h_high = h_part(half, tiles - half)
-    e_part, gi, h_low, h_high, w = lax.optimization_barrier((e_part, gi, h_low, h_high, w))
-
-    for bit in col_bits[1:]:
-        e_part = halve(e_part, permute_row, bit).astype(BF16)
+    e_own, gi, h_low, h_high, w = lax.optimization_barrier((e_own, gi[0], h_low, h_high, w))
+
     h_high = halve(h_high, permute_col, 1).astype(BF16)
-    gi = row_sum(gi, row_bits[1:2])
+    gi = row_sum(gi, row_bits[:2])
     for bit in col_bits[1:]:
         h_low = halve(h_low.astype(BF16), permute_col, bit)
     updated = update(0, some, [])
-    e_part, gi, h_high, updated, w = lax.optimization_barrier((e_part, gi, h_high, updated, w))
+    gi, h_high, updated, w = lax.optimization_barrier((gi, h_high, updated, w))
 
     for bit in col_bits[1:]:
         h_high = halve(h_high.astype(BF16), permute_col, bit)
-    e_own = sum_all([transpose(e_part[m], m, back=True) for m in range(groups)])
     for bit in row_bits[2:]:
         gi = row_sum(gi.astype(BF16), [bit])
     updated = update(some, tiles - some, [updated])
-    h_low, h_high, e_own, gi, updated = lax.optimization_barrier((h_low, h_high, e_own, gi, updated))
+    h_low, h_high, gi, updated = lax.optimization_barrier((h_low, h_high, gi, updated))
     h = jnp.concatenate([h_low[0], h_high[0]], 0)
     grad_panel = jnp.concatenate([h[:slots] + e_own, h[slots:]], 0)
     updated = updated.reshape(tiles, tile, tile // LANES, slabs, LANES).transpose(0, 1, 3, 2, 4)

time: 60.6 us -> 64.5 us (1.064)
  starting transfers between devices: 23.9 us -> 27.4 us
  Pallas kernels: 22 us -> 24.2 us
  local copies, waits for them, and re-layouts: 1.23 us -> 0.13 us
  waiting for transfers between devices: 9.33 us -> 8.64 us
    ppermute x7 -> x10, starting transfers between devices: 8.04 us -> 12 us  [permute_row(): return lax.ppermute(value, 'row', [(i, i ^ bit) for i in range(n_row)])]
    ppermute x4, starting transfers between devices: 10.5 us -> 7.9 us  [transpose(): return lax.ppermute(value, BOTH, pairs)]
    ppermute x4, waiting for transfers between devices: 0.01 us -> 2.26 us  [transpose(): return lax.ppermute(value, BOTH, pairs)]
    ppermute x10 -> x9, starting transfers between devices: 5.35 us -> 7.51 us  [permute_col(): return lax.ppermute(value, 'col', [(i, i ^ bit) for i in range(n_col)])]
    ppermute x7 -> x10, waiting for transfers between devices: 6.57 us -> 4.44 us  [permute_row(): return lax.ppermute(value, 'row', [(i, i ^ bit) for i in range(n_row)])]
    pallas_call x1 -> x2, Pallas kernels: 6.01 us -> 7.81 us  [unmix(): pl.pallas_call(functools.partial(unmix_kernel, slabs, tile, first), grid=...]
    unnamed x8, local copies, waits for them, and re-layouts: 1.12 us -> 0.02 us
    ppermute x10 -> x9, waiting for transfers between devices: 2.75 us -> 1.95 us  [permute_col(): return lax.ppermute(value, 'col', [(i, i ^ bit) for i in range(n_col)])]
  transfers between devices with their start and end apart: 21 -> 23, of which waited for: 7 -> 5; matrix products, arithmetic and copies ran while one was open for 2% -> 1% of each run, Pallas kernels for 36% -> 35%
where the time goes in v1:
time: 64.5 us; the launch traced here: 64.2 us
  starting transfers between devices  27.4 us (42%)
  Pallas kernels  24.2 us (38%)
  waiting for transfers between devices  8.64 us (13%)
  other arithmetic  2.99 us (5%)
  between operations  0.96 us (1%)
    ppermute x10, starting transfers between devices, permute_row(): return lax.ppermute(value, 'row', [(i, i ^ bit) for i in range(n_row)])  12 us
    ppermute x4, starting transfers between devices, transpose(): return lax.ppermute(value, BOTH, pairs)  7.9 us
    pallas_call x2, Pallas kernels, unmix(): pl.pallas_call(functools.partial(unmix_kernel, slabs, tile, first), grid=...  7.81 us
    ppermute x9, starting transfers between devices, permute_col(): return lax.ppermute(value, 'col', [(i, i ^ bit) for i in range(n_col)])  7.51 us
    pallas_call x2, Pallas kernels, update(): pl.pallas_call(functools.partial(update_kernel, slabs, tile), grid=(count...  6.28 us
    pallas_call x1, Pallas kernels, per_device(): pl.pallas_call(functools.partial(q_kernel, n_row, n_col, groups), grid=(s...  4.46 us
    ppermute x10, waiting for transfers between devices, permute_row(): return lax.ppermute(value, 'row', [(i, i ^ bit) for i in range(n_row)])  4.44 us
    pallas_call x2, Pallas kernels, h_part(): pl.pallas_call(functools.partial(h_kernel, n_col), grid=(count,), in_spec...  3.93 us
  transfers between devices with their start and end apart: 23, of which 5 were waited for; matrix products, arithmetic and copies ran while one was open for 1% of the time, Pallas kernels for 35%

profile of v1, /device:TPU:0, one launch (start us, length us, event | category | flops | bytes accessed | tf_op | source)
XLA Modules:
  0.0 64.2 jit_solution(15553003241722798307)
XLA Ops:
  0.6 1.1 %fusion.2.refs_0_ = bf16[8,64,256]{2,1,0:T(8,128)(2,1)S(1)} fusion(f32[8,1,256,64]{2,3,1,0:T(8,128)} %param.4), kind=kLoop, calls=%fused_computation.7 | loop fusion | flops 131072 | bytes 786432 | tf_op jit(solution)/shard_map/convert_element_type | solution.py:205
  1.7 3.0 %collective-permute-start.3 = (bf16[8,64,256]{2,1,0:T(8,128)(2,1)S(1)}, bf16[8,64,256]{2,1,0:T(8,128)(2,1)S(1)}, u32[]{:S(2)}, u32[]{:S(2)}) collective-permute-start(bf16[8,64,256]{2,1,0:T(8,128)(2,1)S(1)} %fusion.2.refs_0_), channel_id=1, source_target_pairs={{0,2},{1,3},{2,0},{3,1},{4,6},{5,7},{6,4},{7,5},{8,10},{9,11},{10,... | collective-permute-start | bytes 786440 | tf_op jit(solution)/shard_map/ppermute | solution.py:191
  4.7 3.7 %collective-permute-start.1 = (bf16[2,64,256]{2,1,0:T(8,128)(2,1)S(1)}, bf16[2,64,256]{2,1,0:T(8,128)(2,1)S(1)}, u32[]{:S(2)}, u32[]{:S(2)}) collective-permute-start(bf16[2,64,256]{2,1,0:T(8,128)(2,1)S(1)} %slice.89), channel_id=1, source_target_pairs={{0,24},{1,28},{2,16},{3,20},{4,25},{5,29},{6,17},{7,21},{8,26},{9,... | collective-permute-start | bytes 196616 | tf_op jit(solution)/shard_map/ppermute | solution.py:203
  8.4 0.5 collective-permute-start
  8.9 4.7 %shard_map.67 = (bf16[2048,1024]{1,0:T(8,128)(2,1)}, bf16[2,256,256]{2,1,0:T(8,128)(2,1)}) custom-call(f32[256,256]{1,0:T(8,128)} %refs_5_.1, bf16[16384,128]{1,0:T(8,128)(2,1)} %bitcast.55), custom_call_target="tpu_custom_call" | custom-call | bytes 4194304 | tf_op jit(solution)/shard_map/pallas_call | solution.py:212
  14.0 0.9 %collective-permute-start.4 = (bf16[8,64,256]{2,1,0:T(8,128)(2,1)S(1)}, bf16[8,64,256]{2,1,0:T(8,128)(2,1)S(1)}, u32[]{:S(2)}, u32[]{:S(2)}) collective-permute-start(bf16[8,64,256]{2,1,0:T(8,128)(2,1)S(1)} %collective-permute-done.3.refs_2_), channel_id=1, source_target_pairs={{0,1},{1,0},{2,3},{3,2},{4,5},{5,4},{6,7},{7,6},{8,9},{9,8},{10,11... | collective-permute-start | bytes 786440 | tf_op jit(solution)/shard_map/ppermute | solution.py:191
  14.9 1.0 %collective-permute-start.10 = (bf16[2,2,64,256]{3,2,1,0:T(8,128)(2,1)S(1)}, bf16[2,2,64,256]{3,2,1,0:T(8,128)(2,1)S(1)}, u32[]{:S(2)}, u32[]{:S(2)}) collective-permute-start(bf16[2,2,64,256]{3,2,1,0:T(8,128)(2,1)S(1)} %pad_maximum_fusion.1.refs_0_), channel_id=1, source_target_pairs={{0,12},{4,8},{8,4},{12,0},{16,28},{20,24},{24,20},{28,16},{1,13},{... | collective-permute-start | bytes 393224 | tf_op jit(solution)/shard_map/ppermute | solution.py:188
  15.8 1.6 %collective-permute-start.9 = (bf16[2,2,64,256]{3,2,1,0:T(8,128)(2,1)S(1)}, bf16[2,2,64,256]{3,2,1,0:T(8,128)(2,1)S(1)}, u32[]{:S(2)}, u32[]{:S(2)}) collective-permute-start(bf16[2,2,64,256]{3,2,1,0:T(8,128)(2,1)S(1)} %pad_maximum_fusion.1.refs_0_), channel_id=1, source_target_pairs={{0,8},{4,12},{8,0},{12,4},{16,24},{20,28},{24,16},{28,20},{1,9},{5... | collective-permute-start | bytes 393224 | tf_op jit(solution)/shard_map/ppermute | solution.py:188
  17.5 1.0 %collective-permute-start.8 = (bf16[2,2,64,256]{3,2,1,0:T(8,128)(2,1)S(1)}, bf16[2,2,64,256]{3,2,1,0:T(8,128)(2,1)S(1)}, u32[]{:S(2)}, u32[]{:S(2)}) collective-permute-start(bf16[2,2,64,256]{3,2,1,0:T(8,128)(2,1)S(1)} %pad_maximum_fusion.1.refs_0_), channel_id=1, source_target_pairs={{0,4},{4,0},{8,12},{12,8},{16,20},{20,16},{24,28},{28,24},{1,5},{5... | collective-permute-start | bytes 393224 | tf_op jit(solution)/shard_map/ppermute | solution.py:188
  18.5 3.1 %shard_map.68.refs_5_.g_ref = bf16[2048,1024]{1,0:T(8,128)(2,1)} custom-call(bf16[16384,128]{1,0:T(8,128)(2,1)} %bitcast.56, bf16[2048,1024]{1,0:T(8,128)(2,1)} %get-tuple-element.38.refs_1_), custom_call_target="tpu_custom_call", output_to_operand_aliasing={{}: (1, {})} | custom-call | bytes 4194304 | tf_op jit(solution)/shard_map/pallas_call | solution.py:212
  21.7 4.5 %shard_map.69 = (bf16[4,256,256]{2,1,0:T(8,128)(2,1)S(1)}, bf16[4,2,2,64,256]{4,3,2,1,0:T(8,128)(2,1)S(1)}, bf16[256,2048]{1,0:T(8,128)(2,1)S(1)}) custom-call(s32[2]{0:T(128)S(1)} %pad_add_fusion.place_ref, bf16[8,64,256]{2,1,0:T(8,128)(2,1)S(1)} %fusion.2.refs_0_, bf16[8,64,256]{2,1,0:T(8,128)(2,1)S(1)} %collective-permute-done.2.refs_1_, ...), custom_call_target="tpu_custom_call" | custom-call | flops 1073741824 | bytes 5242880 | tf_op jit(solution)/shard_map/pallas_call | solution.py:247
  26.2 1.7 %shard_map.70 = (bf16[256,1024]{1,0:T(8,128)(2,1)S(1)}, bf16[4,64,256]{2,1,0:T(8,128)(2,1)S(1)}) custom-call(s32[2]{0:T(128)S(1)} %pad_add_fusion.place_ref, bf16[2,2,64,256]{3,2,1,0:T(8,128)(2,1)S(1)} %pad_maximum_fusion.1.refs_0_, bf16[2,2,64,256]{3,2,1,0:T(8,128)(2,1)S(1)} %collective-permute-done.8.refs_1_, ...), custom_call_target="tpu_custom_call" | custom-call | flops 256 | bytes 256 | tf_op jit(solution)/shard_map/pallas_call | solution.py:272
  28.0 1.1 %collective-permute-start.5 = (bf16[2,2,64,256]{3,2,1,0:T(8,128)(2,1)S(1)}, bf16[2,2,64,256]{3,2,1,0:T(8,128)(2,1)S(1)}, u32[]{:S(2)}, u32[]{:S(2)}) collective-permute-start(bf16[2,2,64,256]{3,2,1,0:T(8,128)(2,1)S(1)} %get-tuple-element.66), channel_id=1, source_target_pairs={{0,4},{4,0},{8,12},{12,8},{16,20},{20,16},{24,28},{28,24},{1,5},{5... | collective-permute-start | bytes 393224 | tf_op jit(solution)/shard_map/ppermute | solution.py:188
  29.1 0.6 collective-permute-start.7
  29.7 1.8 %collective-permute-start.6 = (bf16[2,2,64,256]{3,2,1,0:T(8,128)(2,1)S(1)}, bf16[2,2,64,256]{3,2,1,0:T(8,128)(2,1)S(1)}, u32[]{:S(2)}, u32[]{:S(2)}) collective-permute-start(bf16[2,2,64,256]{3,2,1,0:T(8,128)(2,1)S(1)} %get-tuple-element.68), channel_id=1, source_target_pairs={{0,8},{4,12},{8,0},{12,4},{16,24},{20,28},{24,16},{28,20},{1,9},{5... | collective-permute-start | bytes 393224 | tf_op jit(solution)/shard_map/ppermute | solution.py:188
  31.5 2.0 %shard_map.71 = bf16[4,4,64,256]{3,2,1,0:T(8,128)(2,1)S(1)} custom-call(s32[2]{0:T(128)S(1)} %pad_add_fusion.place_ref, bf16[256,1024]{1,0:T(8,128)(2,1)S(1)} %get-tuple-element.56.w_ref, bf16[2048,1024]{1,0:T(8,128)(2,1)S(1)} %copy-done), custom_call_target="tpu_custom_call" | custom-call | flops 536870912 | bytes 4194304 | tf_op jit(solution)/shard_map/pallas_call | solution.py:286
  33.6 3.2 %collective-permute-done.5 = bf16[2,2,64,256]{3,2,1,0:T(8,128)(2,1)S(1)} collective-permute-done((bf16[2,2,64,256]{3,2,1,0:T(8,128)(2,1)S(1)}, bf16[2,2,64,256]{3,2,1,0:T(8,128)(2,1)S(1)}, u32[]{:S(2)}, u32[]{:S(2)}) %collective-permute-start.5) | collective-permute-done | bytes 131104 | tf_op jit(solution)/shard_map/ppermute | solution.py:188
  36.8 1.2 %collective-permute-done.6 = bf16[2,2,64,256]{3,2,1,0:T(8,128)(2,1)S(1)} collective-permute-done((bf16[2,2,64,256]{3,2,1,0:T(8,128)(2,1)S(1)}, bf16[2,2,64,256]{3,2,1,0:T(8,128)(2,1)S(1)}, u32[]{:S(2)}, u32[]{:S(2)}) %collective-permute-start.6) | collective-permute-done | bytes 131104 | tf_op jit(solution)/shard_map/ppermute | solution.py:188
  38.1 1.5 %collective-permute-start.14 = (bf16[1,64,256]{2,1,0:T(8,128)(2,1)S(1)}, bf16[1,64,256]{2,1,0:T(8,128)(2,1)S(1)}, u32[]{:S(2)}, u32[]{:S(2)}) collective-permute-start(bf16[1,64,256]{2,1,0:T(8,128)(2,1)S(1)} %slice.77), channel_id=1, source_target_pairs={{0,2},{1,3},{2,0},{3,1},{4,6},{5,7},{6,4},{7,5},{8,10},{9,11},{10,... | collective-permute-start | bytes 98312 | tf_op jit(solution)/shard_map/ppermute | solution.py:191
  39.6 0.6 collective-permute-start.12
  40.2 3.1 %collective-permute-start.13 = (bf16[2,64,256]{2,1,0:T(8,128)(2,1)S(1)}, bf16[2,64,256]{2,1,0:T(8,128)(2,1)S(1)}, u32[]{:S(2)}, u32[]{:S(2)}) collective-permute-start(bf16[2,64,256]{2,1,0:T(8,128)(2,1)S(1)} %get-tuple-element.70), channel_id=1, source_target_pairs={{24,0},{28,1},{16,2},{20,3},{25,4},{29,5},{17,6},{21,7},{26,8},{30... | collective-permute-start | bytes 196616 | tf_op jit(solution)/shard_map/ppermute | solution.py:203
  43.4 2.0 %shard_map.72 = bf16[4,4,64,256]{3,2,1,0:T(8,128)(2,1)S(1)} custom-call(s32[2]{0:T(128)S(1)} %pad_add_fusion.place_ref, bf16[256,1024]{1,0:T(8,128)(2,1)S(1)} %get-tuple-element.56.w_ref, bf16[2048,1024]{1,0:T(8,128)(2,1)S(1)} %copy-done), custom_call_target="tpu_custom_call" | custom-call | flops 536870912 | bytes 4194304 | tf_op jit(solution)/shard_map/pallas_call | solution.py:286
  45.4 1.9 %collective-permute-done.13 = bf16[2,64,256]{2,1,0:T(8,128)(2,1)S(1)} collective-permute-done((bf16[2,64,256]{2,1,0:T(8,128)(2,1)S(1)}, bf16[2,64,256]{2,1,0:T(8,128)(2,1)S(1)}, u32[]{:S(2)}, u32[]{:S(2)}) %collective-permute-start.13) | collective-permute-done | bytes 65568 | tf_op jit(solution)/shard_map/ppermute | solution.py:203
  47.8 2.3 %collective-permute-start.18 = (bf16[64,256]{1,0:T(8,128)(2,1)S(1)}, bf16[64,256]{1,0:T(8,128)(2,1)S(1)}, u32[]{:S(2)}, u32[]{:S(2)}) collective-permute-start(bf16[64,256]{1,0:T(8,128)(2,1)S(1)} %fusion.5), channel_id=1, source_target_pairs={{0,8},{4,12},{8,0},{12,4},{16,24},{20,28},{24,16},{28,20},{1,9},{5... | collective-permute-start | bytes 98312 | tf_op jit(solution)/shard_map/ppermute | solution.py:188
  50.1 0.9 %collective-permute-start.17 = (bf16[64,256]{1,0:T(8,128)(2,1)S(1)}, bf16[64,256]{1,0:T(8,128)(2,1)S(1)}, u32[]{:S(2)}, u32[]{:S(2)}) collective-permute-start(bf16[64,256]{1,0:T(8,128)(2,1)S(1)} %fusion.5), channel_id=1, source_target_pairs={{0,4},{4,0},{8,12},{12,8},{16,20},{20,16},{24,28},{28,24},{1,5},{5... | collective-permute-start | bytes 98312 | tf_op jit(solution)/shard_map/ppermute | solution.py:188
  51.5 2.5 %shard_map.73.refs_0_ = bf16[16384,128]{1,0:T(8,128)(2,1)} custom-call(bf16[256,2048]{1,0:T(8,128)(2,1)S(1)} %get-tuple-element.52.pt_ref, bf16[256,1024]{1,0:T(8,128)(2,1)S(1)} %get-tuple-element.56.w_ref, bf16[16384,128]{1,0:T(8,128)(2,1)S(1)} %bitcast.53), custom_call_target="tpu_custom_call" | custom-call | flops 402653184 | bytes 3145728 | tf_op jit(solution)/shard_map/pallas_call | solution.py:301
  54.1 1.9 %collective-permute-done.16 = bf16[1,4,64,256]{3,2,1,0:T(8,128)(2,1)S(1)} collective-permute-done((bf16[1,4,64,256]{3,2,1,0:T(8,128)(2,1)S(1)}, bf16[1,4,64,256]{3,2,1,0:T(8,128)(2,1)S(1)}, u32[]{:S(2)}, u32[]{:S(2)}) %collective-permute-start.16) | collective-permute-done | bytes 131104 | tf_op jit(solution)/shard_map/ppermute | solution.py:191
  56.1 1.3 %collective-permute-start.22 = (bf16[64,256]{1,0:T(8,128)(2,1)S(1)}, bf16[64,256]{1,0:T(8,128)(2,1)S(1)}, u32[]{:S(2)}, u32[]{:S(2)}) collective-permute-start(bf16[64,256]{1,0:T(8,128)(2,1)S(1)} %add_add_fusion), channel_id=1, source_target_pairs={{0,16},{4,20},{8,24},{12,28},{16,0},{20,4},{24,8},{28,12},{1,17},{... | collective-permute-start | bytes 98312 | tf_op jit(solution)/shard_map/ppermute | solution.py:188
  57.5 1.5 %collective-permute-start.21 = (bf16[1,4,64,256]{3,2,1,0:T(8,128)(2,1)S(1)}, bf16[1,4,64,256]{3,2,1,0:T(8,128)(2,1)S(1)}, u32[]{:S(2)}, u32[]{:S(2)}) collective-permute-start(bf16[1,4,64,256]{3,2,1,0:T(8,128)(2,1)S(1)} %slice.85), channel_id=1, source_target_pairs={{0,2},{1,3},{2,0},{3,1},{4,6},{5,7},{6,4},{7,5},{8,10},{9,11},{10,... | collective-permute-start | bytes 393224 | tf_op jit(solution)/shard_map/ppermute | solution.py:191
  58.9 3.8 %shard_map.74 = bf16[16384,128]{1,0:T(8,128)(2,1)} custom-call(bf16[256,2048]{1,0:T(8,128)(2,1)S(1)} %get-tuple-element.52.pt_ref, bf16[256,1024]{1,0:T(8,128)(2,1)S(1)} %get-tuple-element.56.w_ref, bf16[16384,128]{1,0:T(8,128)(2,1)S(1)} %bitcast.54, bf16[16384,128]{1,0:T(8,128)(2,1)} %shard_map.73.refs_0_), custom_call_target="tpu_custom_call", output_to_operand_aliasing={{}: (3, {})} | custom-call | flops 671088640 | bytes 5242880 | tf_op jit(solution)/shard_map/pallas_call | solution.py:301
  62.7 0.6 convert_add_fusion.4
  63.4 0.8 %fusion.1 = f32[8,1,256,64]{2,3,1,0:T(8,128)} fusion(f32[4,64,256]{2,1,0:T(8,128)S(1)} %bitcast.59, f32[4,64,256]{2,1,0:T(8,128)S(1)} %bitcast.58, f32[2,64,256]{2,1,0:T(8,128)S(1)} %bitcast_add_fusion), kind=kLoop, calls=%fused_computation.2 | loop fusion | flops 524288 | bytes 1179648
  (54 shorter events, 2.1 us)
Async XLA Ops:
  1.7 12.3 %collective-permute-start.3 = (bf16[8,64,256]{2,1,0:T(8,128)(2,1)S(1)}, bf16[8,64,256]{2,1,0:T(8,128)(2,1)S(1)}, u32[]{:S(2)}, u32[]{:S(2)}) collective-permute-start(bf16[8,64,256]{2,1,0:T(8,128)(2,1)S(1)} %fusion.2.refs_0_), channel_id=1, source_target_pairs={{0,2},{1,3},{2,0},{3,1},{4,6},{5,7},{6,4},{7,5},{8,10},{9,11},{10,... | collective-permute-start | bytes 786440 | tf_op jit(solution)/shard_map/ppermute | solution.py:191
  4.7 9.3 %collective-permute-start.2 = (bf16[8,64,256]{2,1,0:T(8,128)(2,1)S(1)}, bf16[8,64,256]{2,1,0:T(8,128)(2,1)S(1)}, u32[]{:S(2)}, u32[]{:S(2)}) collective-permute-start(bf16[8,64,256]{2,1,0:T(8,128)(2,1)S(1)} %fusion.2.refs_0_), channel_id=1, source_target_pairs={{0,1},{1,0},{2,3},{3,2},{4,5},{5,4},{6,7},{7,6},{8,9},{9,8},{10,11... | collective-permute-start | bytes 786440 | tf_op jit(solution)/shard_map/ppermute | solution.py:191
  4.7 8.9 %collective-permute-start.1 = (bf16[2,64,256]{2,1,0:T(8,128)(2,1)S(1)}, bf16[2,64,256]{2,1,0:T(8,128)(2,1)S(1)}, u32[]{:S(2)}, u32[]{:S(2)}) collective-permute-start(bf16[2,64,256]{2,1,0:T(8,128)(2,1)S(1)} %slice.89), channel_id=1, source_target_pairs={{0,24},{1,28},{2,16},{3,20},{4,25},{5,29},{6,17},{7,21},{8,26},{9,... | collective-permute-start | bytes 196616 | tf_op jit(solution)/shard_map/ppermute | solution.py:203
  8.4 5.6 %collective-permute-start = (bf16[2,64,256]{2,1,0:T(8,128)(2,1)S(1)}, bf16[2,64,256]{2,1,0:T(8,128)(2,1)S(1)}, u32[]{:S(2)}, u32[]{:S(2)}) collective-permute-start(bf16[2,64,256]{2,1,0:T(8,128)(2,1)S(1)} %slice.89), channel_id=1, source_target_pairs={{0,8},{1,12},{2,0},{3,4},{4,9},{5,13},{6,1},{7,5},{8,10},{9,14},{1... | collective-permute-start | bytes 196616 | tf_op jit(solution)/shard_map/ppermute | solution.py:203
  14.0 7.6 %collective-permute-start.4 = (bf16[8,64,256]{2,1,0:T(8,128)(2,1)S(1)}, bf16[8,64,256]{2,1,0:T(8,128)(2,1)S(1)}, u32[]{:S(2)}, u32[]{:S(2)}) collective-permute-start(bf16[8,64,256]{2,1,0:T(8,128)(2,1)S(1)} %collective-permute-done.3.refs_2_), channel_id=1, source_target_pairs={{0,1},{1,0},{2,3},{3,2},{4,5},{5,4},{6,7},{7,6},{8,9},{9,8},{10,11... | collective-permute-start | bytes 786440 | tf_op jit(solution)/shard_map/ppermute | solution.py:191
  14.9 11.2 %collective-permute-start.10 = (bf16[2,2,64,256]{3,2,1,0:T(8,128)(2,1)S(1)}, bf16[2,2,64,256]{3,2,1,0:T(8,128)(2,1)S(1)}, u32[]{:S(2)}, u32[]{:S(2)}) collective-permute-start(bf16[2,2,64,256]{3,2,1,0:T(8,128)(2,1)S(1)} %pad_maximum_fusion.1.refs_0_), channel_id=1, source_target_pairs={{0,12},{4,8},{8,4},{12,0},{16,28},{20,24},{24,20},{28,16},{1,13},{... | collective-permute-start | bytes 393224 | tf_op jit(solution)/shard_map/ppermute | solution.py:188
  15.8 10.3 %collective-permute-start.9 = (bf16[2,2,64,256]{3,2,1,0:T(8,128)(2,1)S(1)}, bf16[2,2,64,256]{3,2,1,0:T(8,128)(2,1)S(1)}, u32[]{:S(2)}, u32[]{:S(2)}) collective-permute-start(bf16[2,2,64,256]{3,2,1,0:T(8,128)(2,1)S(1)} %pad_maximum_fusion.1.refs_0_), channel_id=1, source_target_pairs={{0,8},{4,12},{8,0},{12,4},{16,24},{20,28},{24,16},{28,20},{1,9},{5... | collective-permute-start | bytes 393224 | tf_op jit(solution)/shard_map/ppermute | solution.py:188
  17.5 8.7 %collective-permute-start.8 = (bf16[2,2,64,256]{3,2,1,0:T(8,128)(2,1)S(1)}, bf16[2,2,64,256]{3,2,1,0:T(8,128)(2,1)S(1)}, u32[]{:S(2)}, u32[]{:S(2)}) collective-permute-start(bf16[2,2,64,256]{3,2,1,0:T(8,128)(2,1)S(1)} %pad_maximum_fusion.1.refs_0_), channel_id=1, source_target_pairs={{0,4},{4,0},{8,12},{12,8},{16,20},{20,16},{24,28},{28,24},{1,5},{5... | collective-permute-start | bytes 393224 | tf_op jit(solution)/shard_map/ppermute | solution.py:188
  18.5 3.1 %copy-start.3 = (bf16[2,256,256]{2,1,0:T(8,128)(2,1)S(1)}, bf16[2,256,256]{2,1,0:T(8,128)(2,1)}, u32[]{:S(2)}) copy-start(bf16[2,256,256]{2,1,0:T(8,128)(2,1)} %get-tuple-element.37.refs_4_) | copy-start | bytes 786436
  21.6 4.5 %copy-start.2 = (f32[256,256]{1,0:T(8,128)S(1)}, f32[256,256]{1,0:T(8,128)}, u32[]{:S(2)}) copy-start(f32[256,256]{1,0:T(8,128)} %refs_5_.1) | copy-start | bytes 786436
  21.6 9.9 %copy-start = (bf16[2048,1024]{1,0:T(8,128)(2,1)S(1)}, bf16[2048,1024]{1,0:T(8,128)(2,1)}, u32[]{:S(2)}) copy-start(bf16[2048,1024]{1,0:T(8,128)(2,1)} %shard_map.68.refs_5_.g_ref) | copy-start | bytes 12582916
  27.9 5.6 %collective-permute-start.11 = (bf16[2,64,256]{2,1,0:T(8,128)(2,1)S(1)}, bf16[2,64,256]{2,1,0:T(8,128)(2,1)S(1)}, u32[]{:S(2)}, u32[]{:S(2)}) collective-permute-start(bf16[2,64,256]{2,1,0:T(8,128)(2,1)S(1)} %slice.73), channel_id=1, source_target_pairs={{0,1},{1,0},{2,3},{3,2},{4,5},{5,4},{6,7},{7,6},{8,9},{9,8},{10,11... | collective-permute-start | bytes 196616 | tf_op jit(solution)/shard_map/ppermute | solution.py:191
  28.0 8.8 %collective-permute-start.5 = (bf16[2,2,64,256]{3,2,1,0:T(8,128)(2,1)S(1)}, bf16[2,2,64,256]{3,2,1,0:T(8,128)(2,1)S(1)}, u32[]{:S(2)}, u32[]{:S(2)}) collective-permute-start(bf16[2,2,64,256]{3,2,1,0:T(8,128)(2,1)S(1)} %get-tuple-element.66), channel_id=1, source_target_pairs={{0,4},{4,0},{8,12},{12,8},{16,20},{20,16},{24,28},{28,24},{1,5},{5... | collective-permute-start | bytes 393224 | tf_op jit(solution)/shard_map/ppermute | solution.py:188
  29.1 7.7 %collective-permute-start.7 = (bf16[2,2,64,256]{3,2,1,0:T(8,128)(2,1)S(1)}, bf16[2,2,64,256]{3,2,1,0:T(8,128)(2,1)S(1)}, u32[]{:S(2)}, u32[]{:S(2)}) collective-permute-start(bf16[2,2,64,256]{3,2,1,0:T(8,128)(2,1)S(1)} %get-tuple-element.67), channel_id=1, source_target_pairs={{0,12},{4,8},{8,4},{12,0},{16,28},{20,24},{24,20},{28,16},{1,13},{... | collective-permute-start | bytes 393224 | tf_op jit(solution)/shard_map/ppermute | solution.py:188
  29.7 8.3 %collective-permute-start.6 = (bf16[2,2,64,256]{3,2,1,0:T(8,128)(2,1)S(1)}, bf16[2,2,64,256]{3,2,1,0:T(8,128)(2,1)S(1)}, u32[]{:S(2)}, u32[]{:S(2)}) collective-permute-start(bf16[2,2,64,256]{3,2,1,0:T(8,128)(2,1)S(1)} %get-tuple-element.68), channel_id=1, source_target_pairs={{0,8},{4,12},{8,0},{12,4},{16,24},{20,28},{24,16},{28,20},{1,9},{5... | collective-permute-start | bytes 393224 | tf_op jit(solution)/shard_map/ppermute | solution.py:188
  33.6 18.0 %copy-start.1 = (bf16[8,1,256,4,1,256]{5,3,4,2,1,0:T(4,128)(2,1)S(1)}, bf16[8,1,256,4,1,256]{5,3,4,2,1,0:T(4,128)(2,1)}, u32[]{:S(2)}) copy-start(bf16[8,1,256,4,1,256]{5,3,4,2,1,0:T(4,128)(2,1)} %param.5) | copy-start | bytes 12582916
  38.1 7.3 %collective-permute-start.14 = (bf16[1,64,256]{2,1,0:T(8,128)(2,1)S(1)}, bf16[1,64,256]{2,1,0:T(8,128)(2,1)S(1)}, u32[]{:S(2)}, u32[]{:S(2)}) collective-permute-start(bf16[1,64,256]{2,1,0:T(8,128)(2,1)S(1)} %slice.77), channel_id=1, source_target_pairs={{0,2},{1,3},{2,0},{3,1},{4,6},{5,7},{6,4},{7,5},{8,10},{9,11},{10,... | collective-permute-start | bytes 98312 | tf_op jit(solution)/shard_map/ppermute | solution.py:191
  39.6 5.8 %collective-permute-start.12 = (bf16[2,64,256]{2,1,0:T(8,128)(2,1)S(1)}, bf16[2,64,256]{2,1,0:T(8,128)(2,1)S(1)}, u32[]{:S(2)}, u32[]{:S(2)}) collective-permute-start(bf16[2,64,256]{2,1,0:T(8,128)(2,1)S(1)} %get-tuple-element.69), channel_id=1, source_target_pairs={{8,0},{12,1},{0,2},{4,3},{9,4},{13,5},{1,6},{5,7},{10,8},{14,9},{2... | collective-permute-start | bytes 196616 | tf_op jit(solution)/shard_map/ppermute | solution.py:203
  40.2 7.1 %collective-permute-start.13 = (bf16[2,64,256]{2,1,0:T(8,128)(2,1)S(1)}, bf16[2,64,256]{2,1,0:T(8,128)(2,1)S(1)}, u32[]{:S(2)}, u32[]{:S(2)}) collective-permute-start(bf16[2,64,256]{2,1,0:T(8,128)(2,1)S(1)} %get-tuple-element.70), channel_id=1, source_target_pairs={{24,0},{28,1},{16,2},{20,3},{25,4},{29,5},{17,6},{21,7},{26,8},{30... | collective-permute-start | bytes 196616 | tf_op jit(solution)/shard_map/ppermute | solution.py:203
  43.3 4.0 %collective-permute-start.15 = (bf16[2,4,64,256]{3,2,1,0:T(8,128)(2,1)S(1)}, bf16[2,4,64,256]{3,2,1,0:T(8,128)(2,1)S(1)}, u32[]{:S(2)}, u32[]{:S(2)}) collective-permute-start(bf16[2,4,64,256]{3,2,1,0:T(8,128)(2,1)S(1)} %slice.79), channel_id=1, source_target_pairs={{0,1},{1,0},{2,3},{3,2},{4,5},{5,4},{6,7},{7,6},{8,9},{9,8},{10,11... | collective-permute-start | bytes 786440 | tf_op jit(solution)/shard_map/ppermute | solution.py:191
  47.4 6.6 %collective-permute-start.19 = (bf16[64,256]{1,0:T(8,128)(2,1)S(1)}, bf16[64,256]{1,0:T(8,128)(2,1)S(1)}, u32[]{:S(2)}, u32[]{:S(2)}) collective-permute-start(bf16[64,256]{1,0:T(8,128)(2,1)S(1)} %fusion.5), channel_id=1, source_target_pairs={{0,12},{4,8},{8,4},{12,0},{16,28},{20,24},{24,20},{28,16},{1,13},{... | collective-permute-start | bytes 98312 | tf_op jit(solution)/shard_map/ppermute | solution.py:188
  47.8 6.2 %collective-permute-start.18 = (bf16[64,256]{1,0:T(8,128)(2,1)S(1)}, bf16[64,256]{1,0:T(8,128)(2,1)S(1)}, u32[]{:S(2)}, u32[]{:S(2)}) collective-permute-start(bf16[64,256]{1,0:T(8,128)(2,1)S(1)} %fusion.5), channel_id=1, source_target_pairs={{0,8},{4,12},{8,0},{12,4},{16,24},{20,28},{24,16},{28,20},{1,9},{5... | collective-permute-start | bytes 98312 | tf_op jit(solution)/shard_map/ppermute | solution.py:188
  50.1 4.0 %collective-permute-start.17 = (bf16[64,256]{1,0:T(8,128)(2,1)S(1)}, bf16[64,256]{1,0:T(8,128)(2,1)S(1)}, u32[]{:S(2)}, u32[]{:S(2)}) collective-permute-start(bf16[64,256]{1,0:T(8,128)(2,1)S(1)} %fusion.5), channel_id=1, source_target_pairs={{0,4},{4,0},{8,12},{12,8},{16,20},{20,16},{24,28},{28,24},{1,5},{5... | collective-permute-start | bytes 98312 | tf_op jit(solution)/shard_map/ppermute | solution.py:188
  51.0 5.0 %collective-permute-start.16 = (bf16[1,4,64,256]{3,2,1,0:T(8,128)(2,1)S(1)}, bf16[1,4,64,256]{3,2,1,0:T(8,128)(2,1)S(1)}, u32[]{:S(2)}, u32[]{:S(2)}) collective-permute-start(bf16[1,4,64,256]{3,2,1,0:T(8,128)(2,1)S(1)} %slice.81), channel_id=1, source_target_pairs={{0,2},{1,3},{2,0},{3,1},{4,6},{5,7},{6,4},{7,5},{8,10},{9,11},{10,... | collective-permute-start | bytes 393224 | tf_op jit(solution)/shard_map/ppermute | solution.py:191
  51.4 4.6 %collective-permute-start.20 = (bf16[2,4,64,256]{3,2,1,0:T(8,128)(2,1)S(1)}, bf16[2,4,64,256]{3,2,1,0:T(8,128)(2,1)S(1)}, u32[]{:S(2)}, u32[]{:S(2)}) collective-permute-start(bf16[2,4,64,256]{3,2,1,0:T(8,128)(2,1)S(1)} %slice.83), channel_id=1, source_target_pairs={{0,1},{1,0},{2,3},{3,2},{4,5},{5,4},{6,7},{7,6},{8,9},{9,8},{10,11... | collective-permute-start | bytes 786440 | tf_op jit(solution)/shard_map/ppermute | solution.py:191
  56.1 6.6 %collective-permute-start.22 = (bf16[64,256]{1,0:T(8,128)(2,1)S(1)}, bf16[64,256]{1,0:T(8,128)(2,1)S(1)}, u32[]{:S(2)}, u32[]{:S(2)}) collective-permute-start(bf16[64,256]{1,0:T(8,128)(2,1)S(1)} %add_add_fusion), channel_id=1, source_target_pairs={{0,16},{4,20},{8,24},{12,28},{16,0},{20,4},{24,8},{28,12},{1,17},{... | collective-permute-start | bytes 98312 | tf_op jit(solution)/shard_map/ppermute | solution.py:188
  57.5 5.9 %collective-permute-start.21 = (bf16[1,4,64,256]{3,2,1,0:T(8,128)(2,1)S(1)}, bf16[1,4,64,256]{3,2,1,0:T(8,128)(2,1)S(1)}, u32[]{:S(2)}, u32[]{:S(2)}) collective-permute-start(bf16[1,4,64,256]{3,2,1,0:T(8,128)(2,1)S(1)} %slice.85), channel_id=1, source_target_pairs={{0,2},{1,3},{2,0},{3,1},{4,6},{5,7},{6,4},{7,5},{8,10},{9,11},{10,... | collective-permute-start | bytes 393224 | tf_op jit(solution)/shard_map/ppermute | solution.py:191

commit v2 on v0

--- a/solution.py
+++ b/solution.py
@@ -45,7 +45,7 @@
     return pl.CostEstimate(flops=flops, bytes_accessed=nbytes, transcendentals=0)
 
 
-def unmix_kernel(slabs, tile, inv_ref, x_ref, o_ref, m_ref, wide_ref, ins, outs, in_sems, out_sems):
+def unmix_kernel(slabs, tile, x_ref, o_ref, token_ref, wide_ref, ins, outs, in_sems, out_sems):
     step, steps = pl.program_id(0), ins.shape[0]
     size = ins.shape[1]
 
@@ -61,10 +61,7 @@
     def _():
         for t in range(steps):
             copy_in(t).start()
-        mat = dot(inv_ref[...], inv_ref[...], ((0,), (0,)), lax.Precision.HIGHEST)
-        high = mat.astype(BF16)
-        m_ref[0] = high
-        m_ref[1] = (mat - high.astype(F32)).astype(BF16)
+        token_ref[...] = jnp.zeros_like(token_ref)
 
     copy_in(step).wait()
     halves = tile // LANES
@@ -82,7 +79,7 @@
 
 
 def q_kernel(n_row, n_col, groups, place_ref, *refs):
-    parts, (m_ref, g_ref, q_ref, e_ref, pt_ref, ins, sems) = refs[:n_col], refs[n_col:]
+    parts, (inv_ref, g_ref, q_ref, e_ref, pt_ref, m_ref, ins, sems) = refs[:n_col], refs[n_col:]
     tiles, strip, tile = parts[0].shape
     s = pl.program_id(0)
     row, col = place_ref[0], place_ref[1]
@@ -96,6 +93,10 @@
     def _():
         for at in range(ins.shape[0]):
             copy_in(at).start()
+        mat = dot(inv_ref[...], inv_ref[...], ((0,), (0,)), lax.Precision.HIGHEST)
+        high = mat.astype(BF16)
+        m_ref[0] = high
+        m_ref[1] = (mat - high.astype(F32)).astype(BF16)
         for q in range(n_col):
             at = pl.multiple_of((col ^ q) * strip, strip)
             for t in range(tiles):
@@ -112,28 +113,27 @@
             e_val = e_val.astype(BF16)
             slot, other = at // groups, group ^ (at % groups)
             for r in range(n_col):
-                place = reversed_bits(rho ^ r, n_col) * groups + other
-                e_ref[place, slot] = e_val[r * strip : (r + 1) * strip]
+                e_ref[reversed_bits(rho ^ r, n_col), other, slot] = e_val[r * strip : (r + 1) * strip]
 
 
 def w_kernel(n_row, n_col, groups, place_ref, *refs):
-    tops, (m_ref, inv_ref, q_ref, w_ref, gi_ref, top_all) = refs[:2], refs[2:]
+    tops, (m_ref, inv_ref, q_ref, _, w_ref, wt_ref, gi_ref, top_all) = refs[:n_col], refs[n_col:]
     slots, strip, tile = tops[0].shape[1:]
-    half = tops[0].shape[0]
     slabs = slots * groups
     row, col = place_ref[0], place_ref[1]
     group, rho = row // n_col, (row % n_col) ^ (n_col // 2)
     for p in range(n_row):
         at = pl.multiple_of((rho ^ (p % n_col)) * strip, strip)
-        place = reversed_bits(p % n_col, n_col) * groups + p // n_col
         for slot in range(slots):
             s = slot * groups + (group ^ (p // n_col))
-            top_all[s, pl.ds(at, strip), :] = tops[place // half][place % half, slot]
+            top_all[s, pl.ds(at, strip), :] = tops[p % n_col][p // n_col, slot]
     z = jnp.zeros((tile, tile), F32)
     for s in range(slabs):
         top = top_all[s]
         w = dot(m_ref[0], top, ((1,), (0,))) + dot(m_ref[1], top, ((1,), (0,)))
-        w_ref[:, s * tile : (s + 1) * tile] = w.astype(BF16)
+        w = w.astype(BF16)
+        w_ref[:, s * tile : (s + 1) * tile] = w
+        wt_ref[s * tile : (s + 1) * tile, :] = w.T
         z = z + dot(top, q_ref[s], ((1,), (1,)))
     z = z + z.T
     gi = -dot(z, inv_ref[...], ((1,), (1,)), lax.Precision.HIGHEST)
@@ -141,13 +141,14 @@
         gi_ref[col ^ r] = gi[r * strip : (r + 1) * strip].astype(BF16)
 
 
-def h_kernel(n_col, place_ref, w_ref, g_ref, h_ref):
+def h_kernel(n_col, place_ref, wt_ref, g_ref, h_ref):
     strip = h_ref.shape[2]
     t = pl.program_id(0)
     col = place_ref[1]
-    h = -dot(w_ref[...], g_ref[...], ((1,), (1,)))
+    h = -dot(g_ref[...], wt_ref[...], ((1,), (0,)))
+    h = h.astype(BF16).T
     for r in range(n_col):
-        h_ref[reversed_bits(col ^ r, n_col), t] = h[r * strip : (r + 1) * strip].astype(BF16)
+        h_ref[reversed_bits(col ^ r, n_col), t] = h[r * strip : (r + 1) * strip]
 
 
 def update_kernel(slabs, tile, pt_ref, w_ref, x_ref, *refs):
@@ -199,16 +200,19 @@
 
     own = panel.reshape(tiles, tile, strip).transpose(0, 2, 1).astype(BF16)
     high, *lower = bits_of(n_col)
+    half = tiles // 2
     parts = {0: own, high: permute_col(own, high)}
+    if lower:
+        parts[1] = permute_col(own, 1)
     tops = [transpose(own[:slots], m) for m in range(groups)]
-    cot, mat = pl.pallas_call(
+    cot, token = pl.pallas_call(
         functools.partial(unmix_kernel, slabs, tile),
         grid=(tiles,),
-        in_specs=[whole((tile, tile)), ANY],
-        out_specs=[ANY, whole((2, tile, tile))],
+        in_specs=[ANY],
+        out_specs=[ANY, whole((8, LANES))],
         out_shape=[
             jax.ShapeDtypeStruct((rows, width), BF16),
-            jax.ShapeDtypeStruct((2, tile, tile), BF16),
+            jax.ShapeDtypeStruct((8, LANES), F32),
         ],
         scratch_shapes=[
             pltpu.VMEM((mixed, LANES), F32),
@@ -219,38 +223,34 @@
         ],
         compiler_params=params(STREAMED),
         cost_estimate=cost(0, 4 * rows * width),
-    )(inverse, mixed_rows(cotangent))
-
-    tops, own, mat = lax.optimization_barrier((tops, own, mat))
+    )(mixed_rows(cotangent))
+
+    tops, parts, token = lax.optimization_barrier((tops, parts, token))
 
     top = jnp.stack(tops)
-    for bit in bits_of(n_col)[:-1]:
-        top = jnp.concatenate([top, permute_row(top, bit)], 0)
-    if lower:
-        parts[1] = permute_col(own, 1)
-    top, parts = lax.optimization_barrier((top, parts))
-
+    tops = [top] + [permute_row(top, q) for q in range(1, n_col)]
     for bit in lower:
         for q in range(0, n_col, 2 * bit):
             if q | bit not in parts:
                 parts[q | bit] = permute_col(parts[q], bit)
-    tops = [top, permute_row(top, 1)]
-
-    q_sum, e_part, panel_all = pl.pallas_call(
+
+    q_sum, e_part, panel_all, mat = pl.pallas_call(
         functools.partial(q_kernel, n_row, n_col, groups),
         grid=(slabs,),
         in_specs=[SMEM]
         + [whole((tiles, strip, tile))] * n_col
-        + [whole((2, tile, tile)), ANY],
+        + [whole((tile, tile)), ANY],
         out_specs=[
             whole((slabs, tile, tile)),
-            whole((n_row, slots, strip, tile)),
+            whole((n_col, groups, slots, strip, tile)),
             whole((tile, rows)),
+            whole((2, tile, tile)),
         ],
         out_shape=[
             jax.ShapeDtypeStruct((slabs, tile, tile), BF16),
-            jax.ShapeDtypeStruct((n_row, slots, strip, tile), BF16),
+            jax.ShapeDtypeStruct((n_col, groups, slots, strip, tile), BF16),
             jax.ShapeDtypeStruct((tile, rows), BF16),
+            jax.ShapeDtypeStruct((2, tile, tile), BF16),
         ],
         scratch_shapes=[
             pltpu.VMEM((slabs, rows, tile), BF16),
@@ -258,20 +258,21 @@
         ],
         compiler_params=params(STREAMED - 10),
         cost_estimate=cost(2 * rows * width * tile, 2 * rows * (width + tile)),
-    )(place, *[parts[q] for q in range(n_col)], mat, cot)
-
-    w, gi = pl.pallas_call(
+    )(place, *[parts[q] for q in range(n_col)], inverse, cot)
+
+    w, w_flip, gi = pl.pallas_call(
         functools.partial(w_kernel, n_row, n_col, groups),
-        in_specs=[SMEM] + [VMEM] * 5,
-        out_specs=[VMEM, VMEM],
+        in_specs=[SMEM] + [VMEM] * (n_col + 3) + [ANY],
+        out_specs=[VMEM, VMEM, VMEM],
         out_shape=[
             jax.ShapeDtypeStruct((tile, width), BF16),
+            jax.ShapeDtypeStruct((width, tile), BF16),
             jax.ShapeDtypeStruct((n_col, strip, tile), BF16),
         ],
         scratch_shapes=[pltpu.VMEM((slabs, tile, tile), BF16)],
         compiler_params=params(),
         cost_estimate=cost(tile, tile),
-    )(place, *tops, mat, inverse, q_sum)
+    )(place, *tops, mat, inverse, q_sum, token)
 
     def h_part(first, count):
         return pl.pallas_call(
@@ -279,14 +280,14 @@
             grid=(count,),
             in_specs=[
                 SMEM,
-                whole((tile, width)),
+                whole((width, tile)),
                 pl.BlockSpec((tile, width), lambda t: (t + first, 0)),
             ],
             out_specs=whole((n_col, count, strip, tile)),
             out_shape=jax.ShapeDtypeStruct((n_col, count, strip, tile), BF16),
             compiler_params=params(),
             cost_estimate=cost(tile, tile),
-        )(place, w, cot)
+        )(place, w_flip, cot)
 
     def update(first, count, previous):
         return pl.pallas_call(
@@ -321,12 +322,11 @@
         return sum_all([value] + [permute_row(value, step) for step in steps[1:]])
 
     col_bits, row_bits = list(reversed(bits_of(n_col))), list(reversed(bits_of(n_row)))
-    half = tiles // 2
-    some = tiles * 3 // 8
+    some = tiles // 2
     e_part = halve(e_part, permute_row, 1).astype(BF16)
     gi = sum_all([gi[0]] + [permute_col(gi[q], q) for q in range(1, n_col)]).astype(BF16)
     h_low = h_part(0, half)
-    e_part, gi, h_low, w = lax.optimization_barrier((e_part, gi, h_low, w))
+    e_part, gi, h_low, w, w_flip = lax.optimization_barrier((e_part, gi, h_low, w, w_flip))
 
     gi = row_sum(gi, row_bits[:1]).astype(BF16)
     h_low = halve(h_low, permute_col, 1).astype(BF16)
@@ -344,7 +344,7 @@
 
     for bit in col_bits[1:]:
         h_high = halve(h_high.astype(BF16), permute_col, bit)
-    e_own = sum_all([transpose(e_part[m], m, back=True) for m in range(groups)])
+    e_own = sum_all([transpose(e_part[0, m], m, back=True) for m in range(groups)])
     for bit in row_bits[2:]:
         gi = row_sum(gi.astype(BF16), [bit])
     updated = update(some, tiles - some, [updated])

time: 60.6 us -> 55 us (0.908)
  waiting for transfers between devices: 9.33 us -> 4.1 us
  starting transfers between devices: 23.9 us -> 25.7 us
  Pallas kernels: 22 us -> 20.9 us
  local copies, waits for them, and re-layouts: 1.23 us -> 0.13 us
    ppermute x4, starting transfers between devices: 10.5 us -> 6.64 us  [transpose(): return lax.ppermute(value, BOTH, pairs)]
    ppermute x7 -> x8, waiting for transfers between devices: 6.57 us -> 2.81 us  [permute_row(): return lax.ppermute(value, 'row', [(i, i ^ bit) for i in range(n_row)])]
    ppermute x10, starting transfers between devices: 5.35 us -> 8.91 us  [permute_col(): return lax.ppermute(value, 'col', [(i, i ^ bit) for i in range(n_col)])]
    ppermute x7 -> x8, starting transfers between devices: 8.04 us -> 10.2 us  [permute_row(): return lax.ppermute(value, 'row', [(i, i ^ bit) for i in range(n_row)])]
    ppermute x10, waiting for transfers between devices: 2.75 us -> 0.72 us  [permute_col(): return lax.ppermute(value, 'col', [(i, i ^ bit) for i in range(n_col)])]
    unnamed x8, local copies, waits for them, and re-layouts: 1.12 us -> 0.02 us
    pallas_call x1, Pallas kernels: 6.01 us -> 4.92 us  [per_device(): pl.pallas_call(functools.partial(unmix_kernel, slabs, tile), grid=(tiles,...]
  transfers between devices with their start and end apart: 21 -> 22, of which waited for: 7 -> 7; matrix products, arithmetic and copies ran while one was open for 2% -> 2% of each run, Pallas kernels for 36% -> 38%
where the time goes in v2:
time: 55 us; the launch traced here: 54.8 us
  starting transfers between devices  25.7 us (47%)
  Pallas kernels  20.9 us (38%)
  waiting for transfers between devices  4.1 us (7%)
  other arithmetic  3.05 us (6%)
  between operations  0.87 us (2%)
    ppermute x8, starting transfers between devices, permute_row(): return lax.ppermute(value, 'row', [(i, i ^ bit) for i in range(n_row)])  10.2 us
    ppermute x10, starting transfers between devices, permute_col(): return lax.ppermute(value, 'col', [(i, i ^ bit) for i in range(n_col)])  8.91 us
    ppermute x4, starting transfers between devices, transpose(): return lax.ppermute(value, BOTH, pairs)  6.64 us
    pallas_call x2, Pallas kernels, update(): pl.pallas_call(functools.partial(update_kernel, slabs, tile), grid=(count...  5.95 us
    pallas_call x1, Pallas kernels, per_device(): pl.pallas_call(functools.partial(unmix_kernel, slabs, tile), grid=(tiles,...  4.92 us
    pallas_call x2, Pallas kernels, h_part(): pl.pallas_call(functools.partial(h_kernel, n_col), grid=(count,), in_spec...  4.23 us
    pallas_call x1, Pallas kernels, per_device(): pl.pallas_call(functools.partial(q_kernel, n_row, n_col, groups), grid=(s...  4.16 us
    ppermute x8, waiting for transfers between devices, permute_row(): return lax.ppermute(value, 'row', [(i, i ^ bit) for i in range(n_row)])  2.81 us
  transfers between devices with their start and end apart: 22, of which 7 were waited for; matrix products, arithmetic and copies ran while one was open for 2% of the time, Pallas kernels for 38%

profile of v2, /device:TPU:0, one launch (start us, length us, event | category | flops | bytes accessed | tf_op | source)
XLA Modules:
  0.0 54.8 jit_solution(8167429772101463451)
XLA Ops:
  0.6 1.1 %fusion.2.refs_0_ = bf16[8,64,256]{2,1,0:T(8,128)(2,1)S(1)} fusion(f32[8,1,256,64]{2,3,1,0:T(8,128)} %param.4), kind=kLoop, calls=%fused_computation.8 | loop fusion | flops 131072 | bytes 786432 | tf_op jit(solution)/shard_map/convert_element_type | solution.py:201
  1.8 0.5 collective-permute-start.2
  2.3 2.6 %collective-permute-start.3 = (bf16[8,64,256]{2,1,0:T(8,128)(2,1)S(1)}, bf16[8,64,256]{2,1,0:T(8,128)(2,1)S(1)}, u32[]{:S(2)}, u32[]{:S(2)}) collective-permute-start(bf16[8,64,256]{2,1,0:T(8,128)(2,1)S(1)} %fusion.2.refs_0_), channel_id=1, source_target_pairs={{0,2},{1,3},{2,0},{3,1},{4,6},{5,7},{6,4},{7,5},{8,10},{9,11},{10,... | collective-permute-start | bytes 786440 | tf_op jit(solution)/shard_map/ppermute | solution.py:187
  4.8 1.6 %collective-permute-start = (bf16[2,64,256]{2,1,0:T(8,128)(2,1)S(1)}, bf16[2,64,256]{2,1,0:T(8,128)(2,1)S(1)}, u32[]{:S(2)}, u32[]{:S(2)}) collective-permute-start(bf16[2,64,256]{2,1,0:T(8,128)(2,1)S(1)} %slice.89), channel_id=1, source_target_pairs={{0,8},{1,12},{2,0},{3,4},{4,9},{5,13},{6,1},{7,5},{8,10},{9,14},{1... | collective-permute-start | bytes 196616 | tf_op jit(solution)/shard_map/ppermute | solution.py:199
  6.4 2.6 %collective-permute-start.1 = (bf16[2,64,256]{2,1,0:T(8,128)(2,1)S(1)}, bf16[2,64,256]{2,1,0:T(8,128)(2,1)S(1)}, u32[]{:S(2)}, u32[]{:S(2)}) collective-permute-start(bf16[2,64,256]{2,1,0:T(8,128)(2,1)S(1)} %slice.89), channel_id=1, source_target_pairs={{0,24},{1,28},{2,16},{3,20},{4,25},{5,29},{6,17},{7,21},{8,26},{9,... | collective-permute-start | bytes 196616 | tf_op jit(solution)/shard_map/ppermute | solution.py:199
  9.0 4.9 %shard_map.67 = (bf16[2048,1024]{1,0:T(8,128)(2,1)}, f32[8,128]{1,0:T(8,128)}) custom-call(bf16[16384,128]{1,0:T(8,128)(2,1)} %bitcast.54), custom_call_target="tpu_custom_call" | custom-call | bytes 8388608 | tf_op jit(solution)/shard_map/pallas_call | solution.py:208
  13.9 0.6 %collective-permute-done.1 = bf16[2,64,256]{2,1,0:T(8,128)(2,1)S(1)} collective-permute-done((bf16[2,64,256]{2,1,0:T(8,128)(2,1)S(1)}, bf16[2,64,256]{2,1,0:T(8,128)(2,1)S(1)}, u32[]{:S(2)}, u32[]{:S(2)}) %collective-permute-start.1) | collective-permute-done | bytes 65568 | tf_op jit(solution)/shard_map/ppermute | solution.py:199
  14.5 1.2 %collective-permute-start.4 = (bf16[8,64,256]{2,1,0:T(8,128)(2,1)S(1)}, bf16[8,64,256]{2,1,0:T(8,128)(2,1)S(1)}, u32[]{:S(2)}, u32[]{:S(2)}) collective-permute-start(bf16[8,64,256]{2,1,0:T(8,128)(2,1)S(1)} %collective-permute-done.3.refs_2_), channel_id=1, source_target_pairs={{0,1},{1,0},{2,3},{3,2},{4,5},{5,4},{6,7},{7,6},{8,9},{9,8},{10,11... | collective-permute-start | bytes 786440 | tf_op jit(solution)/shard_map/ppermute | solution.py:187
  15.7 0.6 %collective-permute-start.6 = (bf16[2,2,64,256]{3,2,1,0:T(8,128)(2,1)S(1)}, bf16[2,2,64,256]{3,2,1,0:T(8,128)(2,1)S(1)}, u32[]{:S(2)}, u32[]{:S(2)}) collective-permute-start(bf16[2,2,64,256]{3,2,1,0:T(8,128)(2,1)S(1)} %pad_maximum_fusion.1.refs_0_), channel_id=1, source_target_pairs={{0,4},{4,0},{8,12},{12,8},{16,20},{20,16},{24,28},{28,24},{1,5},{5... | collective-permute-start | bytes 393224 | tf_op jit(solution)/shard_map/ppermute | solution.py:184
  16.3 0.8 %collective-permute-start.7 = (bf16[2,2,64,256]{3,2,1,0:T(8,128)(2,1)S(1)}, bf16[2,2,64,256]{3,2,1,0:T(8,128)(2,1)S(1)}, u32[]{:S(2)}, u32[]{:S(2)}) collective-permute-start(bf16[2,2,64,256]{3,2,1,0:T(8,128)(2,1)S(1)} %pad_maximum_fusion.1.refs_0_), channel_id=1, source_target_pairs={{0,8},{4,12},{8,0},{12,4},{16,24},{20,28},{24,16},{28,20},{1,9},{5... | collective-permute-start | bytes 393224 | tf_op jit(solution)/shard_map/ppermute | solution.py:184
  17.1 2.1 %collective-permute-start.8 = (bf16[2,2,64,256]{3,2,1,0:T(8,128)(2,1)S(1)}, bf16[2,2,64,256]{3,2,1,0:T(8,128)(2,1)S(1)}, u32[]{:S(2)}, u32[]{:S(2)}) collective-permute-start(bf16[2,2,64,256]{3,2,1,0:T(8,128)(2,1)S(1)} %pad_maximum_fusion.1.refs_0_), channel_id=1, source_target_pairs={{0,12},{4,8},{8,4},{12,0},{16,28},{20,24},{24,20},{28,16},{1,13},{... | collective-permute-start | bytes 393224 | tf_op jit(solution)/shard_map/ppermute | solution.py:184
  19.3 4.2 %shard_map.68 = (bf16[4,256,256]{2,1,0:T(8,128)(2,1)S(1)}, bf16[4,2,2,64,256]{4,3,2,1,0:T(8,128)(2,1)S(1)}, bf16[256,2048]{1,0:T(8,128)(2,1)S(1)}, bf16[2,256,256]{2,1,0:T(8,128)(2,1)S(1)}) custom-call(s32[2]{0:T(128)S(1)} %pad_add_fusion.place_ref, bf16[8,64,256]{2,1,0:T(8,128)(2,1)S(1)} %fusion.2.refs_0_, ...), custom_call_target="tpu_custom_call" | custom-call | flops 1073741824 | bytes 5242880 | tf_op jit(solution)/shard_map/pallas_call | solution.py:237
  23.5 0.6 %collective-permute-start.5 = (bf16[2,2,2,64,256]{4,3,2,1,0:T(8,128)(2,1)S(1)}, bf16[2,2,2,64,256]{4,3,2,1,0:T(8,128)(2,1)S(1)}, u32[]{:S(2)}, u32[]{:S(2)}) collective-permute-start(bf16[2,2,2,64,256]{4,3,2,1,0:T(8,128)(2,1)S(1)} %slice.69), channel_id=1, source_target_pairs={{0,4},{4,0},{8,12},{12,8},{16,20},{20,16},{24,28},{28,24},{1,5},{5... | collective-permute-start | bytes 786440 | tf_op jit(solution)/shard_map/ppermute | solution.py:184
  24.1 1.1 %collective-permute-done.8.refs_3_ = bf16[2,2,64,256]{3,2,1,0:T(8,128)(2,1)S(1)} collective-permute-done((bf16[2,2,64,256]{3,2,1,0:T(8,128)(2,1)S(1)}, bf16[2,2,64,256]{3,2,1,0:T(8,128)(2,1)S(1)}, u32[]{:S(2)}, u32[]{:S(2)}) %collective-permute-start.8) | collective-permute-done | bytes 131104 | tf_op jit(solution)/shard_map/ppermute | solution.py:184
  25.2 1.7 %shard_map.69 = (bf16[256,1024]{1,0:T(8,128)(2,1)S(1)}, bf16[1024,256]{1,0:T(8,128)(2,1)S(1)}, bf16[4,64,256]{2,1,0:T(8,128)(2,1)S(1)}) custom-call(s32[2]{0:T(128)S(1)} %pad_add_fusion.place_ref, bf16[2,2,64,256]{3,2,1,0:T(8,128)(2,1)S(1)} %pad_maximum_fusion.1.refs_0_, bf16[2,2,64,256]{3,2,1,0:T(8,128)(2,1)S(1)} %collective-permute-done.6.refs_1_, ...), custom_call_target="tpu_custom_call" | custom-call | flops 256 | bytes 256 | tf_op jit(solution)/shard_map/pallas_call | solution.py:263
  26.9 1.4 %collective-permute-start.10 = (bf16[64,256]{1,0:T(8,128)(2,1)S(1)}, bf16[64,256]{1,0:T(8,128)(2,1)S(1)}, u32[]{:S(2)}, u32[]{:S(2)}) collective-permute-start(bf16[64,256]{1,0:T(8,128)(2,1)S(1)} %get-tuple-element.80), channel_id=1, source_target_pairs={{0,2},{1,3},{2,0},{3,1},{4,6},{5,7},{6,4},{7,5},{8,10},{9,11},{10,... | collective-permute-start | bytes 98312 | tf_op jit(solution)/shard_map/ppermute | solution.py:187
  28.3 0.8 %collective-permute-start.9 = (bf16[64,256]{1,0:T(8,128)(2,1)S(1)}, bf16[64,256]{1,0:T(8,128)(2,1)S(1)}, u32[]{:S(2)}, u32[]{:S(2)}) collective-permute-start(bf16[64,256]{1,0:T(8,128)(2,1)S(1)} %get-tuple-element.78), channel_id=1, source_target_pairs={{0,1},{1,0},{2,3},{3,2},{4,5},{5,4},{6,7},{7,6},{8,9},{9,8},{10,11... | collective-permute-start | bytes 98312 | tf_op jit(solution)/shard_map/ppermute | solution.py:187
  29.1 2.1 %shard_map.70 = bf16[4,4,64,256]{3,2,1,0:T(8,128)(2,1)S(1)} custom-call(s32[2]{0:T(128)S(1)} %pad_add_fusion.place_ref, bf16[1024,256]{1,0:T(8,128)(2,1)S(1)} %get-tuple-element.55.wt_ref, bf16[2048,1024]{1,0:T(8,128)(2,1)S(1)} %copy-done), custom_call_target="tpu_custom_call" | custom-call | flops 256 | bytes 256 | tf_op jit(solution)/shard_map/pallas_call | solution.py:278
  31.9 1.2 %collective-permute-start.12 = (bf16[64,256]{1,0:T(8,128)(2,1)S(1)}, bf16[64,256]{1,0:T(8,128)(2,1)S(1)}, u32[]{:S(2)}, u32[]{:S(2)}) collective-permute-start(bf16[64,256]{1,0:T(8,128)(2,1)S(1)} %fusion.4), channel_id=1, source_target_pairs={{0,4},{4,0},{8,12},{12,8},{16,20},{20,16},{24,28},{28,24},{1,5},{5... | collective-permute-start | bytes 98312 | tf_op jit(solution)/shard_map/ppermute | solution.py:184
  33.1 2.1 %shard_map.71 = bf16[4,4,64,256]{3,2,1,0:T(8,128)(2,1)S(1)} custom-call(s32[2]{0:T(128)S(1)} %pad_add_fusion.place_ref, bf16[1024,256]{1,0:T(8,128)(2,1)S(1)} %get-tuple-element.55.wt_ref, bf16[2048,1024]{1,0:T(8,128)(2,1)S(1)} %copy-done), custom_call_target="tpu_custom_call" | custom-call | flops 256 | bytes 256 | tf_op jit(solution)/shard_map/pallas_call | solution.py:278
  35.2 0.6 %collective-permute-done.12 = bf16[64,256]{1,0:T(8,128)(2,1)S(1)} collective-permute-done((bf16[64,256]{1,0:T(8,128)(2,1)S(1)}, bf16[64,256]{1,0:T(8,128)(2,1)S(1)}, u32[]{:S(2)}, u32[]{:S(2)}) %collective-permute-start.12) | collective-permute-done | bytes 32800 | tf_op jit(solution)/shard_map/ppermute | solution.py:184
  36.0 1.8 %collective-permute-start.16 = (bf16[64,256]{1,0:T(8,128)(2,1)S(1)}, bf16[64,256]{1,0:T(8,128)(2,1)S(1)}, u32[]{:S(2)}, u32[]{:S(2)}) collective-permute-start(bf16[64,256]{1,0:T(8,128)(2,1)S(1)} %add_convert_fusion.4), channel_id=1, source_target_pairs={{0,8},{4,12},{8,0},{12,4},{16,24},{20,28},{24,16},{28,20},{1,9},{5... | collective-permute-start | bytes 98312 | tf_op jit(solution)/shard_map/ppermute | solution.py:184
  38.2 1.2 %collective-permute-start.14 = (bf16[1,4,64,256]{3,2,1,0:T(8,128)(2,1)S(1)}, bf16[1,4,64,256]{3,2,1,0:T(8,128)(2,1)S(1)}, u32[]{:S(2)}, u32[]{:S(2)}) collective-permute-start(bf16[1,4,64,256]{3,2,1,0:T(8,128)(2,1)S(1)} %slice.77), channel_id=1, source_target_pairs={{0,2},{1,3},{2,0},{3,1},{4,6},{5,7},{6,4},{7,5},{8,10},{9,11},{10,... | collective-permute-start | bytes 393224 | tf_op jit(solution)/shard_map/ppermute | solution.py:187
  39.4 3.0 %shard_map.72.refs_0_ = bf16[16384,128]{1,0:T(8,128)(2,1)} custom-call(bf16[256,2048]{1,0:T(8,128)(2,1)S(1)} %get-tuple-element.61.pt_ref, bf16[256,1024]{1,0:T(8,128)(2,1)S(1)} %get-tuple-element.66.w_ref, bf16[16384,128]{1,0:T(8,128)(2,1)S(1)} %bitcast.51), custom_call_target="tpu_custom_call" | custom-call | flops 536870912 | bytes 4194304 | tf_op jit(solution)/shard_map/pallas_call | solution.py:293
  42.4 1.1 %collective-permute-done.15 = bf16[1,2,2,64,256]{4,3,2,1,0:T(8,128)(2,1)S(1)} collective-permute-done((bf16[1,2,2,64,256]{4,3,2,1,0:T(8,128)(2,1)S(1)}, bf16[1,2,2,64,256]{4,3,2,1,0:T(8,128)(2,1)S(1)}, u32[]{:S(2)}, u32[]{:S(2)}) %collective-permute-start.15) | collective-permute-done | bytes 131104 | tf_op jit(solution)/shard_map/ppermute | solution.py:184
  43.7 2.7 %collective-permute-start.21 = (bf16[64,256]{1,0:T(8,128)(2,1)S(1)}, bf16[64,256]{1,0:T(8,128)(2,1)S(1)}, u32[]{:S(2)}, u32[]{:S(2)}) collective-permute-start(bf16[64,256]{1,0:T(8,128)(2,1)S(1)} %convert_add_fusion.5), channel_id=1, source_target_pairs={{0,16},{4,20},{8,24},{12,28},{16,0},{20,4},{24,8},{28,12},{1,17},{... | collective-permute-start | bytes 98312 | tf_op jit(solution)/shard_map/ppermute | solution.py:184
  46.4 1.2 %collective-permute-start.19 = (bf16[2,64,256]{2,1,0:T(8,128)(2,1)S(1)}, bf16[2,64,256]{2,1,0:T(8,128)(2,1)S(1)}, u32[]{:S(2)}, u32[]{:S(2)}) collective-permute-start(bf16[2,64,256]{2,1,0:T(8,128)(2,1)S(1)} %get-tuple-element.76), channel_id=1, source_target_pairs={{8,0},{12,1},{0,2},{4,3},{9,4},{13,5},{1,6},{5,7},{10,8},{14,9},{2... | collective-permute-start | bytes 196616 | tf_op jit(solution)/shard_map/ppermute | solution.py:199
  47.5 1.4 %collective-permute-start.20 = (bf16[2,64,256]{2,1,0:T(8,128)(2,1)S(1)}, bf16[2,64,256]{2,1,0:T(8,128)(2,1)S(1)}, u32[]{:S(2)}, u32[]{:S(2)}) collective-permute-start(bf16[2,64,256]{2,1,0:T(8,128)(2,1)S(1)} %get-tuple-element.77), channel_id=1, source_target_pairs={{24,0},{28,1},{16,2},{20,3},{25,4},{29,5},{17,6},{21,7},{26,8},{30... | collective-permute-start | bytes 196616 | tf_op jit(solution)/shard_map/ppermute | solution.py:199
  48.9 1.1 %collective-permute-start.18 = (bf16[1,4,64,256]{3,2,1,0:T(8,128)(2,1)S(1)}, bf16[1,4,64,256]{3,2,1,0:T(8,128)(2,1)S(1)}, u32[]{:S(2)}, u32[]{:S(2)}) collective-permute-start(bf16[1,4,64,256]{3,2,1,0:T(8,128)(2,1)S(1)} %slice.83), channel_id=1, source_target_pairs={{0,2},{1,3},{2,0},{3,1},{4,6},{5,7},{6,4},{7,5},{8,10},{9,11},{10,... | collective-permute-start | bytes 393224 | tf_op jit(solution)/shard_map/ppermute | solution.py:187
  50.0 3.0 %shard_map.73 = bf16[16384,128]{1,0:T(8,128)(2,1)} custom-call(bf16[256,2048]{1,0:T(8,128)(2,1)S(1)} %get-tuple-element.61.pt_ref, bf16[256,1024]{1,0:T(8,128)(2,1)S(1)} %get-tuple-element.66.w_ref, bf16[16384,128]{1,0:T(8,128)(2,1)S(1)} %bitcast.52, bf16[16384,128]{1,0:T(8,128)(2,1)} %shard_map.72.refs_0_), custom_call_target="tpu_custom_call", output_to_operand_aliasing={{}: (3, {})} | custom-call | flops 536870912 | bytes 4194304 | tf_op jit(solution)/shard_map/pallas_call | solution.py:293
  53.0 0.6 %convert_add_fusion.4 = f32[64,256]{1,0:T(8,128)} fusion(bf16[64,256]{1,0:T(8,128)(2,1)S(1)} %collective-permute-done.21, bf16[64,256]{1,0:T(8,128)(2,1)S(1)} %convert_add_fusion.5), kind=kLoop, calls=%fused_computation.18 | loop fusion | flops 49152 | bytes 131072 | tf_op jit(solution)/shard_map/add | solution.py:317
  54.0 0.8 %fusion.1 = f32[8,1,256,64]{2,3,1,0:T(8,128)} fusion(f32[4,64,256]{2,1,0:T(8,128)S(1)} %bitcast.56, f32[4,64,256]{2,1,0:T(8,128)S(1)} %bitcast.55, f32[2,64,256]{2,1,0:T(8,128)S(1)} %bitcast_add_fusion), kind=kLoop, calls=%fused_computation.2 | loop fusion | flops 524288 | bytes 1179648
  (52 shorter events, 1.8 us)
Async XLA Ops:
  0.6 18.7 %copy-start.2 = (f32[256,256]{1,0:T(8,128)S(1)}, f32[256,256]{1,0:T(8,128)}, u32[]{:S(2)}) copy-start(f32[256,256]{1,0:T(8,128)} %refs_5_.1) | copy-start | bytes 786436
  1.8 12.7 %collective-permute-start.2 = (bf16[8,64,256]{2,1,0:T(8,128)(2,1)S(1)}, bf16[8,64,256]{2,1,0:T(8,128)(2,1)S(1)}, u32[]{:S(2)}, u32[]{:S(2)}) collective-permute-start(bf16[8,64,256]{2,1,0:T(8,128)(2,1)S(1)} %fusion.2.refs_0_), channel_id=1, source_target_pairs={{0,1},{1,0},{2,3},{3,2},{4,5},{5,4},{6,7},{7,6},{8,9},{9,8},{10,11... | collective-permute-start | bytes 786440 | tf_op jit(solution)/shard_map/ppermute | solution.py:187
  2.3 12.2 %collective-permute-start.3 = (bf16[8,64,256]{2,1,0:T(8,128)(2,1)S(1)}, bf16[8,64,256]{2,1,0:T(8,128)(2,1)S(1)}, u32[]{:S(2)}, u32[]{:S(2)}) collective-permute-start(bf16[8,64,256]{2,1,0:T(8,128)(2,1)S(1)} %fusion.2.refs_0_), channel_id=1, source_target_pairs={{0,2},{1,3},{2,0},{3,1},{4,6},{5,7},{6,4},{7,5},{8,10},{9,11},{10,... | collective-permute-start | bytes 786440 | tf_op jit(solution)/shard_map/ppermute | solution.py:187
  4.8 9.1 %collective-permute-start = (bf16[2,64,256]{2,1,0:T(8,128)(2,1)S(1)}, bf16[2,64,256]{2,1,0:T(8,128)(2,1)S(1)}, u32[]{:S(2)}, u32[]{:S(2)}) collective-permute-start(bf16[2,64,256]{2,1,0:T(8,128)(2,1)S(1)} %slice.89), channel_id=1, source_target_pairs={{0,8},{1,12},{2,0},{3,4},{4,9},{5,13},{6,1},{7,5},{8,10},{9,14},{1... | collective-permute-start | bytes 196616 | tf_op jit(solution)/shard_map/ppermute | solution.py:199
  6.4 8.1 %collective-permute-start.1 = (bf16[2,64,256]{2,1,0:T(8,128)(2,1)S(1)}, bf16[2,64,256]{2,1,0:T(8,128)(2,1)S(1)}, u32[]{:S(2)}, u32[]{:S(2)}) collective-permute-start(bf16[2,64,256]{2,1,0:T(8,128)(2,1)S(1)} %slice.89), channel_id=1, source_target_pairs={{0,24},{1,28},{2,16},{3,20},{4,25},{5,29},{6,17},{7,21},{8,26},{9,... | collective-permute-start | bytes 196616 | tf_op jit(solution)/shard_map/ppermute | solution.py:199
  13.9 11.3 %copy-start.3 = (f32[8,128]{1,0:T(8,128)S(1)}, f32[8,128]{1,0:T(8,128)}, u32[]{:S(2)}) copy-start(f32[8,128]{1,0:T(8,128)} %get-tuple-element.48.refs_7_) | copy-start | bytes 12292
  14.5 4.8 %collective-permute-start.4 = (bf16[8,64,256]{2,1,0:T(8,128)(2,1)S(1)}, bf16[8,64,256]{2,1,0:T(8,128)(2,1)S(1)}, u32[]{:S(2)}, u32[]{:S(2)}) collective-permute-start(bf16[8,64,256]{2,1,0:T(8,128)(2,1)S(1)} %collective-permute-done.3.refs_2_), channel_id=1, source_target_pairs={{0,1},{1,0},{2,3},{3,2},{4,5},{5,4},{6,7},{7,6},{8,9},{9,8},{10,11... | collective-permute-start | bytes 786440 | tf_op jit(solution)/shard_map/ppermute | solution.py:187
  15.7 13.4 %copy-start = (bf16[2048,1024]{1,0:T(8,128)(2,1)S(1)}, bf16[2048,1024]{1,0:T(8,128)(2,1)}, u32[]{:S(2)}) copy-start(bf16[2048,1024]{1,0:T(8,128)(2,1)} %get-tuple-element.42.refs_5_.g_ref) | copy-start | bytes 12582916
  15.7 8.4 %collective-permute-start.6 = (bf16[2,2,64,256]{3,2,1,0:T(8,128)(2,1)S(1)}, bf16[2,2,64,256]{3,2,1,0:T(8,128)(2,1)S(1)}, u32[]{:S(2)}, u32[]{:S(2)}) collective-permute-start(bf16[2,2,64,256]{3,2,1,0:T(8,128)(2,1)S(1)} %pad_maximum_fusion.1.refs_0_), channel_id=1, source_target_pairs={{0,4},{4,0},{8,12},{12,8},{16,20},{20,16},{24,28},{28,24},{1,5},{5... | collective-permute-start | bytes 393224 | tf_op jit(solution)/shard_map/ppermute | solution.py:184
  16.3 7.8 %collective-permute-start.7 = (bf16[2,2,64,256]{3,2,1,0:T(8,128)(2,1)S(1)}, bf16[2,2,64,256]{3,2,1,0:T(8,128)(2,1)S(1)}, u32[]{:S(2)}, u32[]{:S(2)}) collective-permute-start(bf16[2,2,64,256]{3,2,1,0:T(8,128)(2,1)S(1)} %pad_maximum_fusion.1.refs_0_), channel_id=1, source_target_pairs={{0,8},{4,12},{8,0},{12,4},{16,24},{20,28},{24,16},{28,20},{1,9},{5... | collective-permute-start | bytes 393224 | tf_op jit(solution)/shard_map/ppermute | solution.py:184
  17.1 8.1 %collective-permute-start.8 = (bf16[2,2,64,256]{3,2,1,0:T(8,128)(2,1)S(1)}, bf16[2,2,64,256]{3,2,1,0:T(8,128)(2,1)S(1)}, u32[]{:S(2)}, u32[]{:S(2)}) collective-permute-start(bf16[2,2,64,256]{3,2,1,0:T(8,128)(2,1)S(1)} %pad_maximum_fusion.1.refs_0_), channel_id=1, source_target_pairs={{0,12},{4,8},{8,4},{12,0},{16,28},{20,24},{24,20},{28,16},{1,13},{... | collective-permute-start | bytes 393224 | tf_op jit(solution)/shard_map/ppermute | solution.py:184
  23.5 8.2 %collective-permute-start.5 = (bf16[2,2,2,64,256]{4,3,2,1,0:T(8,128)(2,1)S(1)}, bf16[2,2,2,64,256]{4,3,2,1,0:T(8,128)(2,1)S(1)}, u32[]{:S(2)}, u32[]{:S(2)}) collective-permute-start(bf16[2,2,2,64,256]{4,3,2,1,0:T(8,128)(2,1)S(1)} %slice.69), channel_id=1, source_target_pairs={{0,4},{4,0},{8,12},{12,8},{16,20},{20,16},{24,28},{28,24},{1,5},{5... | collective-permute-start | bytes 786440 | tf_op jit(solution)/shard_map/ppermute | solution.py:184
  26.9 4.3 %collective-permute-start.10 = (bf16[64,256]{1,0:T(8,128)(2,1)S(1)}, bf16[64,256]{1,0:T(8,128)(2,1)S(1)}, u32[]{:S(2)}, u32[]{:S(2)}) collective-permute-start(bf16[64,256]{1,0:T(8,128)(2,1)S(1)} %get-tuple-element.80), channel_id=1, source_target_pairs={{0,2},{1,3},{2,0},{3,1},{4,6},{5,7},{6,4},{7,5},{8,10},{9,11},{10,... | collective-permute-start | bytes 98312 | tf_op jit(solution)/shard_map/ppermute | solution.py:187
  28.3 3.3 %collective-permute-start.11 = (bf16[64,256]{1,0:T(8,128)(2,1)S(1)}, bf16[64,256]{1,0:T(8,128)(2,1)S(1)}, u32[]{:S(2)}, u32[]{:S(2)}) collective-permute-start(bf16[64,256]{1,0:T(8,128)(2,1)S(1)} %get-tuple-element.79), channel_id=1, source_target_pairs={{0,3},{1,2},{2,1},{3,0},{4,7},{5,6},{6,5},{7,4},{8,11},{9,10},{10,... | collective-permute-start | bytes 98312 | tf_op jit(solution)/shard_map/ppermute | solution.py:187
  28.3 3.3 %collective-permute-start.9 = (bf16[64,256]{1,0:T(8,128)(2,1)S(1)}, bf16[64,256]{1,0:T(8,128)(2,1)S(1)}, u32[]{:S(2)}, u32[]{:S(2)}) collective-permute-start(bf16[64,256]{1,0:T(8,128)(2,1)S(1)} %get-tuple-element.78), channel_id=1, source_target_pairs={{0,1},{1,0},{2,3},{3,2},{4,5},{5,4},{6,7},{7,6},{8,9},{9,8},{10,11... | collective-permute-start | bytes 98312 | tf_op jit(solution)/shard_map/ppermute | solution.py:187
  31.7 7.8 %copy-start.1 = (bf16[8,1,256,4,1,256]{5,3,4,2,1,0:T(4,128)(2,1)S(1)}, bf16[8,1,256,4,1,256]{5,3,4,2,1,0:T(4,128)(2,1)}, u32[]{:S(2)}) copy-start(bf16[8,1,256,4,1,256]{5,3,4,2,1,0:T(4,128)(2,1)} %param.5) | copy-start | bytes 12582916
  31.8 4.1 %collective-permute-start.13 = (bf16[2,4,64,256]{3,2,1,0:T(8,128)(2,1)S(1)}, bf16[2,4,64,256]{3,2,1,0:T(8,128)(2,1)S(1)}, u32[]{:S(2)}, u32[]{:S(2)}) collective-permute-start(bf16[2,4,64,256]{3,2,1,0:T(8,128)(2,1)S(1)} %slice.75), channel_id=1, source_target_pairs={{0,1},{1,0},{2,3},{3,2},{4,5},{5,4},{6,7},{7,6},{8,9},{9,8},{10,11... | collective-permute-start | bytes 786440 | tf_op jit(solution)/shard_map/ppermute | solution.py:187
  31.9 4.0 %collective-permute-start.12 = (bf16[64,256]{1,0:T(8,128)(2,1)S(1)}, bf16[64,256]{1,0:T(8,128)(2,1)S(1)}, u32[]{:S(2)}, u32[]{:S(2)}) collective-permute-start(bf16[64,256]{1,0:T(8,128)(2,1)S(1)} %fusion.4), channel_id=1, source_target_pairs={{0,4},{4,0},{8,12},{12,8},{16,20},{20,16},{24,28},{28,24},{1,5},{5... | collective-permute-start | bytes 98312 | tf_op jit(solution)/shard_map/ppermute | solution.py:184
  36.0 7.7 %collective-permute-start.17 = (bf16[2,4,64,256]{3,2,1,0:T(8,128)(2,1)S(1)}, bf16[2,4,64,256]{3,2,1,0:T(8,128)(2,1)S(1)}, u32[]{:S(2)}, u32[]{:S(2)}) collective-permute-start(bf16[2,4,64,256]{3,2,1,0:T(8,128)(2,1)S(1)} %slice.81), channel_id=1, source_target_pairs={{0,1},{1,0},{2,3},{3,2},{4,5},{5,4},{6,7},{7,6},{8,9},{9,8},{10,11... | collective-permute-start | bytes 786440 | tf_op jit(solution)/shard_map/ppermute | solution.py:187
  36.0 6.3 %collective-permute-start.16 = (bf16[64,256]{1,0:T(8,128)(2,1)S(1)}, bf16[64,256]{1,0:T(8,128)(2,1)S(1)}, u32[]{:S(2)}, u32[]{:S(2)}) collective-permute-start(bf16[64,256]{1,0:T(8,128)(2,1)S(1)} %add_convert_fusion.4), channel_id=1, source_target_pairs={{0,8},{4,12},{8,0},{12,4},{16,24},{20,28},{24,16},{28,20},{1,9},{5... | collective-permute-start | bytes 98312 | tf_op jit(solution)/shard_map/ppermute | solution.py:184
  37.9 5.6 %collective-permute-start.15 = (bf16[1,2,2,64,256]{4,3,2,1,0:T(8,128)(2,1)S(1)}, bf16[1,2,2,64,256]{4,3,2,1,0:T(8,128)(2,1)S(1)}, u32[]{:S(2)}, u32[]{:S(2)}) collective-permute-start(bf16[1,2,2,64,256]{4,3,2,1,0:T(8,128)(2,1)S(1)} %slice.79), channel_id=1, source_target_pairs={{0,8},{4,12},{8,0},{12,4},{16,24},{20,28},{24,16},{28,20},{1,9},{5... | collective-permute-start | bytes 393224 | tf_op jit(solution)/shard_map/ppermute | solution.py:184
  38.2 5.4 %collective-permute-start.14 = (bf16[1,4,64,256]{3,2,1,0:T(8,128)(2,1)S(1)}, bf16[1,4,64,256]{3,2,1,0:T(8,128)(2,1)S(1)}, u32[]{:S(2)}, u32[]{:S(2)}) collective-permute-start(bf16[1,4,64,256]{3,2,1,0:T(8,128)(2,1)S(1)} %slice.77), channel_id=1, source_target_pairs={{0,2},{1,3},{2,0},{3,1},{4,6},{5,7},{6,4},{7,5},{8,10},{9,11},{10,... | collective-permute-start | bytes 393224 | tf_op jit(solution)/shard_map/ppermute | solution.py:187
  43.7 9.3 %collective-permute-start.21 = (bf16[64,256]{1,0:T(8,128)(2,1)S(1)}, bf16[64,256]{1,0:T(8,128)(2,1)S(1)}, u32[]{:S(2)}, u32[]{:S(2)}) collective-permute-start(bf16[64,256]{1,0:T(8,128)(2,1)S(1)} %convert_add_fusion.5), channel_id=1, source_target_pairs={{0,16},{4,20},{8,24},{12,28},{16,0},{20,4},{24,8},{28,12},{1,17},{... | collective-permute-start | bytes 98312 | tf_op jit(solution)/shard_map/ppermute | solution.py:184
  46.4 7.3 %collective-permute-start.19 = (bf16[2,64,256]{2,1,0:T(8,128)(2,1)S(1)}, bf16[2,64,256]{2,1,0:T(8,128)(2,1)S(1)}, u32[]{:S(2)}, u32[]{:S(2)}) collective-permute-start(bf16[2,64,256]{2,1,0:T(8,128)(2,1)S(1)} %get-tuple-element.76), channel_id=1, source_target_pairs={{8,0},{12,1},{0,2},{4,3},{9,4},{13,5},{1,6},{5,7},{10,8},{14,9},{2... | collective-permute-start | bytes 196616 | tf_op jit(solution)/shard_map/ppermute | solution.py:199
  47.5 6.1 %collective-permute-start.20 = (bf16[2,64,256]{2,1,0:T(8,128)(2,1)S(1)}, bf16[2,64,256]{2,1,0:T(8,128)(2,1)S(1)}, u32[]{:S(2)}, u32[]{:S(2)}) collective-permute-start(bf16[2,64,256]{2,1,0:T(8,128)(2,1)S(1)} %get-tuple-element.77), channel_id=1, source_target_pairs={{24,0},{28,1},{16,2},{20,3},{25,4},{29,5},{17,6},{21,7},{26,8},{30... | collective-permute-start | bytes 196616 | tf_op jit(solution)/shard_map/ppermute | solution.py:199
  48.9 5.0 %collective-permute-start.18 = (bf16[1,4,64,256]{3,2,1,0:T(8,128)(2,1)S(1)}, bf16[1,4,64,256]{3,2,1,0:T(8,128)(2,1)S(1)}, u32[]{:S(2)}, u32[]{:S(2)}) collective-permute-start(bf16[1,4,64,256]{3,2,1,0:T(8,128)(2,1)S(1)} %slice.83), channel_id=1, source_target_pairs={{0,2},{1,3},{2,0},{3,1},{4,6},{5,7},{6,4},{7,5},{8,10},{9,11},{10,... | collective-permute-start | bytes 393224 | tf_op jit(solution)/shard_map/ppermute | solution.py:187
